TPU v7x, 128 devices: a whole 4x4x4 slice. The times are simulated.
128 devices in a mesh: seq: 16 (over x, y), head: 8 (over z, core).
Axes of the slice: x: 4, y: 4, z: 4, core: 2. Of those that a mesh axis runs over, the one named last changes fastest.
Arguments:
- tokens: bfloat16 [128, 1024, 512], P('head', 'seq'), may hold values from -6 to 6
- lengths: int32 [128], replicated, may hold values from 64 to 1024, as said below
- norm_gain: bfloat16 [512], replicated, may hold values from 0.099609375 to 1.8984375
- value_weight: bfloat16 [512, 512], replicated, may hold values from -0.25 to 0.25
- synth_logits: bfloat16 [8, 1024, 1024], P('head', 'seq'), may hold values from -9 to 9
- out_weight: bfloat16 [512, 512], replicated, may hold values from -1 to 1
- ffn_gain: bfloat16 [512], replicated, may hold values from 0.099609375 to 1.8984375
- up_weight: bfloat16 [512, 2048], replicated, may hold values from -0.25 to 0.25
- down_weight: bfloat16 [2048, 512], replicated, may hold values from -0.125 to 0.125
- cotangent: bfloat16 [128, 1024, 512], P('head', 'seq'), may hold values from -6 to 6
Outputs:
- output: bfloat16 [128, 1024, 512], P('head', 'seq')
- input_grad: float32 [128, 1024, 512], P('head', 'seq')
- norm_gain_grad: float32 [512], replicated
- value_weight_grad: float32 [512, 512], replicated
- synth_logits_grad: float32 [8, 1024, 1024], P('head', 'seq')
- out_weight_grad: float32 [512, 512], replicated
- ffn_gain_grad: float32 [512], replicated
- up_weight_grad: float32 [512, 2048], replicated
- down_weight_grad: float32 [2048, 512], replicated
Inputs may be any that keep to these rules, and one draw needn't show every extreme that they name: `lengths`: among buckets 16 * k to 16 * k + 15 one has length 1024.
All inputs are finite; a program needn't handle non-finite values.
Results may differ from a plain program's by a relative error of at most 0.017.
Values may be sent and summed in bfloat16 or wider, within the bound.
No kernel may reach another device: no remote copies, remote signals or barrier semaphores. Data moves between devices by JAX's collectives and lax.ppermute only.
A program may use at most 256 MiB of HBM per device.

v0:
```python
import math

import jax
import jax.numpy as jnp
from jax import lax
from jax.sharding import PartitionSpec as P

epsilon = 1e-06
root_half = 1.0 / math.sqrt(2.0)
density_norm = 1.0 / math.sqrt(2.0 * math.pi)


def rms_parts(values):
    scale_row = lax.rsqrt(jnp.mean(values * values, axis=-1, keepdims=True) + epsilon)
    return (values * scale_row, scale_row)


def rms_backward(normed, scale_row, gain, grad_hidden):
    weighted = grad_hidden * gain
    back_term = scale_row * (
        weighted - normed * jnp.mean(weighted * normed, axis=-1, keepdims=True)
    )
    return (back_term, jnp.sum(grad_hidden * normed, axis=(0, 1)))


def gelu_parts(pre_act):
    normal_cdf = 0.5 * (1.0 + lax.erf(pre_act * root_half))
    slope = normal_cdf + pre_act * jnp.exp(-0.5 * pre_act * pre_act) * density_norm
    return (pre_act * normal_cdf, slope)


def shards(
    tokens,
    lengths,
    norm_gain,
    value_weight,
    synth_logits,
    out_weight,
    ffn_gain,
    up_weight,
    down_weight,
    cotangent,
):
    group_bkts = tokens.shape[0]
    local_rows = tokens.shape[1]
    width = tokens.shape[2]
    heads_here = synth_logits.shape[0]
    span_len = synth_logits.shape[2]
    bucket_count = lengths.shape[0]
    head_width = width // lax.axis_size("head")
    head_size = head_width // heads_here
    group_index = lax.axis_index("head")
    block_index = lax.axis_index("seq")
    own_lens = lax.dynamic_slice_in_dim(lengths, group_index * group_bkts, group_bkts)
    positions = block_index * local_rows + jnp.arange(local_rows, dtype=jnp.int32)
    row_keep = (positions[None, :] < own_lens[:, None]).astype(jnp.float32)[:, :, None]
    query_keep = (positions[None, :] < lengths[:, None]).astype(jnp.bfloat16)[:, :, None]
    column_keep = (jnp.arange(span_len, dtype=jnp.int32)[None, :] < lengths[:, None]).astype(
        jnp.float32
    )
    logits_f = synth_logits.astype(jnp.float32)
    exponent = jnp.exp(logits_f - jnp.max(logits_f, axis=-1, keepdims=True))
    totals = jnp.einsum("hij,bj->bhi", exponent, column_keep)

    def weights_at():
        return exponent[None] * column_keep[:, None, None, :] / totals[:, :, :, None]

    gain_one = norm_gain.astype(jnp.float32)
    gain_two = ffn_gain.astype(jnp.float32)
    token_f = tokens.astype(jnp.float32)
    normed_one, scale_one = rms_parts(token_f)
    hidden_one = (normed_one * gain_one).astype(jnp.bfloat16)
    values = jnp.dot(hidden_one, value_weight, preferred_element_type=jnp.float32).astype(
        jnp.bfloat16
    )
    head_values = lax.all_to_all(values, "head", split_axis=2, concat_axis=0, tiled=True)
    every_value = lax.all_gather(head_values, "seq", axis=1, tiled=True)
    seg_len = every_value.shape[1]
    weights = weights_at().astype(jnp.bfloat16)
    segment_heads = every_value.reshape(bucket_count, seg_len, heads_here, head_size)
    mixed_heads = jnp.einsum(
        "bhij,bjhd->bihd", weights, segment_heads, preferred_element_type=jnp.float32
    )
    mixed_low = (
        mixed_heads.reshape(bucket_count, local_rows, head_width) * query_keep.astype(jnp.float32)
    ).astype(jnp.bfloat16)
    mixed_tok = lax.all_to_all(mixed_low, "head", split_axis=0, concat_axis=2, tiled=True)
    residual = token_f + jnp.dot(mixed_tok, out_weight, preferred_element_type=jnp.float32)
    normed_two, scale_two = rms_parts(residual)
    hidden_two = (normed_two * gain_two).astype(jnp.bfloat16)
    pre_act = jnp.dot(hidden_two, up_weight, preferred_element_type=jnp.float32)
    active, slope = gelu_parts(pre_act)
    active_low = active.astype(jnp.bfloat16)
    ffn_out = jnp.dot(active_low, down_weight, preferred_element_type=jnp.float32)
    output = ((residual + ffn_out) * row_keep).astype(jnp.bfloat16)
    grad_low = (cotangent.astype(jnp.float32) * row_keep).astype(jnp.bfloat16)
    down_grad = jnp.einsum("gpf,gpd->fd", active_low, grad_low, preferred_element_type=jnp.float32)
    grad_act = jnp.einsum("gpd,fd->gpf", grad_low, down_weight, preferred_element_type=jnp.float32)
    grad_pre = (grad_act * slope).astype(jnp.bfloat16)
    up_grad = jnp.einsum("gpd,gpf->df", hidden_two, grad_pre, preferred_element_type=jnp.float32)
    grad_hidden_two = jnp.einsum(
        "gpf,df->gpd", grad_pre, up_weight, preferred_element_type=jnp.float32
    )
    back_two, ffn_gain_grad = rms_backward(normed_two, scale_two, gain_two, grad_hidden_two)
    grad_resid = grad_low.astype(jnp.float32) + back_two
    grad_att = grad_resid.astype(jnp.bfloat16)
    out_grad = jnp.einsum("gpe,gpd->ed", mixed_tok, grad_att, preferred_element_type=jnp.float32)
    grad_mixed = jnp.einsum(
        "gpd,ed->gpe", grad_att, out_weight, preferred_element_type=jnp.float32
    ).astype(jnp.bfloat16)
    head_grad = lax.all_to_all(grad_mixed, "head", split_axis=2, concat_axis=0, tiled=True)
    masked_grad = head_grad * query_keep
    grad_heads = masked_grad.reshape(bucket_count, local_rows, heads_here, head_size)
    seg_len = every_value.shape[1]
    weights = weights_at()
    segment_heads = every_value.reshape(bucket_count, seg_len, heads_here, head_size)
    prob_grad = jnp.einsum(
        "bihd,bjhd->bhij", grad_heads, segment_heads, preferred_element_type=jnp.float32
    )
    product = weights * prob_grad
    partial_grad = jnp.sum(product, axis=0)
    score_sums = (partial_grad, jnp.sum(product, axis=3))
    partial_grad = score_sums[0]
    row_dots = score_sums[1]
    logits_grad = partial_grad - exponent * jnp.einsum(
        "bhi,bj->hij", row_dots / totals, column_keep
    )
    weights = weights_at().astype(jnp.bfloat16)
    term = jnp.einsum("bhij,bihd->jbhd", weights, grad_heads, preferred_element_type=jnp.float32)
    value_grad = lax.psum_scatter(
        term.reshape(local_rows * lax.axis_size("seq"), bucket_count, head_width).astype(
            jnp.bfloat16
        ),
        "seq",
        scatter_dimension=0,
        tiled=True,
    )
    tok_value_grad = lax.all_to_all(value_grad, "head", split_axis=1, concat_axis=2, tiled=True)
    value_weight_grad = jnp.einsum(
        "gpd,pge->de", hidden_one, tok_value_grad, preferred_element_type=jnp.float32
    )
    grad_hidden_one = jnp.einsum(
        "pge,de->gpd", tok_value_grad, value_weight, preferred_element_type=jnp.float32
    )
    back_one, norm_gain_grad = rms_backward(normed_one, scale_one, gain_one, grad_hidden_one)
    input_grad = grad_resid + back_one
    summed = lax.psum(
        (norm_gain_grad, value_weight_grad, out_grad, ffn_gain_grad, up_grad, down_grad),
        ("seq", "head"),
    )
    return (
        output,
        input_grad,
        summed[0],
        summed[1],
        logits_grad,
        summed[2],
        summed[3],
        summed[4],
        summed[5],
    )


def solution(mesh):
    placed = (
        P("head", "seq", None),
        P(),
        P(),
        P(),
        P("head", "seq", None),
        P(),
        P(),
        P(),
        P(),
        P("head", "seq", None),
    )
    return jax.shard_map(
        shards,
        mesh=mesh,
        in_specs=placed,
        out_specs=(
            P("head", "seq", None),
            P("head", "seq", None),
            P(),
            P(),
            P("head", "seq", None),
            P(),
            P(),
            P(),
            P(),
        ),
        check_vma=False,
    )
```

profile of v0, /device:TPU:1, one launch (start us, length us, event | category | flops | bytes accessed | tf_op | source)
XLA Modules:
  0.0 678.3 jit_solution(5635197218246423629)
XLA Ops:
  7.2 0.8 convert_element_type.101
  8.1 1.5 fusion.27
  9.6 0.6 copy-done.22
  10.2 2.1 convolution_convert_fusion.1
  12.3 2.8 copy.58
  15.2 3.4 reshape.214
  18.5 21.8 %all_to_all.72 = bf16[8,2,32768]{2,1,0:T(2,128)(2,1)} all-to-all(bf16[8,2,32768]{2,1,0:T(2,128)(2,1)S(1)} %reshape.214), channel_id=1, replica_groups=mesh['seq'=16,'head'=8] {'head'}, dimensions={0} | all-to-all | bytes 2097152 | tf_op jit(solution)/shard_map/all_to_all | solution.py:76
  40.3 4.3 reshape.215
  44.6 4.5 copy.59
  49.0 4.1 copy.60
  53.3 0.3 fusion.48
  53.8 0.4 copy-done.20
  54.4 109.9 %all-gather.2.cloned.1.call-done = bf16[128,1024,64]{0,2,1:T(8,128)(2,1)} async-done(((bf16[128,64,64]{0,2,1:T(8,128)(2,1)}), bf16[128,1024,64]{0,2,1:T(8,128)(2,1)}) %all-gather.2.cloned.1.call-update) | async-done | bytes 16777232 | tf_op jit(solution)/shard_map/all_gather | solution.py:77
  164.3 45.5 %copy.73 = bf16[128,1024,64]{2,1,0:T(8,128)(2,1)} copy(bf16[128,1024,64]{0,2,1:T(8,128)(2,1)} %all-gather.2.cloned.1.call-done) | data formatting | bytes 33554432 | tf_op jit(solution)/shard_map/all_gather | solution.py:77
  209.8 15.9 %fusion.57 = bf16[128,64,64]{2,1,0:T(8,128)(2,1)} fusion(f32[128,64]{1,0:T(8,128)S(1)} %get-tuple-element.22, bf16[128,1024,64]{2,1,0:T(8,128)(2,1)} %copy.73, f32[128,64]{1,0:T(8,128)S(1)} %copy.61, f32[128,1024]{1,0:T(8,128)S(1)} %fusion.49, f32[64,1024]{1,0:T(8,128)S(1)} %fusion.52), kind=kOutput, calls=%fused_computation.80 | convolution fusion | flops 1099956224 | bytes 18677760 | tf_op jit(solution)/shard_map/bhij,bjhd->bihd/dot_general | solution.py:81
  225.7 4.3 reshape.216
  230.1 5.1 all-to-all-start.1
  235.5 14.8 %all-to-all-done.1 = bf16[8,2,32768]{2,1,0:T(2,128)(2,1)S(1)} async-done(((bf16[8,2,32768]{2,1,0:T(2,128)(2,1)}), bf16[8,2,32768]{2,1,0:T(2,128)(2,1)S(1)}, u32[]{:S(2)}, u32[]{:S(2)}) %all-to-all-start.1) | async-done | bytes 1048608 | tf_op jit(solution)/shard_map/all_to_all | solution.py:87
  250.3 2.7 reshape.217
  253.0 4.1 copy.63
  257.1 4.1 all_to_all.59
  261.2 2.1 multiply_reduce_fusion.2
  263.4 4.6 multiply_convert_fusion
  268.0 4.5 fusion.13
  272.6 3.2 multiply_reduce_fusion
  275.8 0.7 multiply_add_fusion
  276.5 0.3 copy-done.11
  276.8 1.7 convolution_convert_fusion
  278.5 3.8 copy.64
  282.4 3.4 reshape.218
  285.7 18.5 %all_to_all.73 = bf16[8,2,32768]{2,1,0:T(2,128)(2,1)S(1)} all-to-all(bf16[8,2,32768]{2,1,0:T(2,128)(2,1)S(1)} %reshape.218), channel_id=1, replica_groups=mesh['seq'=16,'head'=8] {'head'}, dimensions={0} | all-to-all | bytes 2097152 | tf_op jit(solution)/shard_map/all_to_all | solution.py:111
  304.3 2.7 reshape.219
  306.9 3.7 copy.65
  310.6 2.4 bitcast_multiply_fusion.2
  313.0 9.6 %convert_bitcast_fusion = bf16[1024,128,64]{0,2,1:T(8,128)(2,1)} fusion(bf16[128,64,64]{2,1,0:T(8,128)(2,1)} %bitcast_multiply_fusion.2, f32[128,64]{1,0:T(8,128)S(1)} %copy.61, f32[128,1024]{1,0:T(8,128)S(1)} %copy-done.19, f32[64,1024]{1,0:T(8,128)S(1)} %fusion.52), kind=kOutput, calls=%fused_computation.3 | convolution fusion | flops 1107296256 | bytes 18644992 | tf_op jit(solution)/shard_map/bhij,bihd->jbhd/dot_general | solution.py:129
  322.6 26.0 %copy.67 = bf16[1024,128,64]{1,2,0:T(8,128)(2,1)} copy(bf16[1024,128,64]{0,2,1:T(8,128)(2,1)} %convert_bitcast_fusion) | data formatting | bytes 33554432 | tf_op jit(solution)/shard_map/convert_element_type | solution.py:131
  348.6 3.8 convolution_bitcast_fusion.2
  352.4 5.6 multiply_convert_fusion.2
  358.1 4.6 convolution_bitcast_fusion.1
  362.7 94.3 %reduce-scatter.2.cloned.1.call-done = bf16[64,128,64]{1,2,0:T(8,128)(2,1)} async-done(((bf16[1024,128,64]{1,2,0:T(8,128)(2,1)}), bf16[64,128,64]{1,2,0:T(8,128)(2,1)}) %reduce-scatter.2.cloned.1.call-update) | async-done | bytes 1048592 | tf_op jit(solution)/shard_map/reduce_scatter | solution.py:130
  457.0 3.9 copy.68
  460.9 2.7 reshape.220
  463.6 5.6 all-to-all-start.3
  469.2 0.2 all-reduce.4.cloned.1.call-start
  469.5 6.7 convolution_bitcast_fusion
  476.2 8.2 %all-to-all-done.3 = bf16[8,2,32768]{2,1,0:T(2,128)(2,1)} async-done(((bf16[8,2,32768]{2,1,0:T(2,128)(2,1)}), bf16[8,2,32768]{2,1,0:T(2,128)(2,1)}, u32[]{:S(2)}, u32[]{:S(2)}) %all-to-all-start.3) | async-done | bytes 1048608 | tf_op jit(solution)/shard_map/all_to_all | solution.py:138
  484.4 3.1 reshape.221
  487.5 3.1 copy.78
  490.6 3.2 reshape.213
  493.9 1.9 convolution_bitcast_fusion.3
  495.8 1.6 copy-done.12
  497.3 17.5 %fusion.56 = (f32[128,64]{1,0:T(8,128)}, f32[64,1024]{1,0:T(8,128)}) fusion(bf16[128,64,64]{2,1,0:T(8,128)(2,1)S(1)} %copy-done.12, bf16[128,1024,64]{2,1,0:T(8,128)(2,1)} %copy.73, f32[128,64]{1,0:T(8,128)} %copy-done.21, f32[128,1024]{1,0:T(8,128)} %copy-done.18, f32[64,1024]{1,0:T(8,128)S(1)} %fusion.52), kind=kOutput, calls=%fused_computation.79 | convolution fusion | flops 1115611136 | bytes 18939904 | tf_op jit(solution)/shard_map/bihd,bjhd->bhij/dot_general | solution.py:117
  514.9 0.9 copy.74
  515.8 2.0 fusion.38
  517.8 3.8 fusion.26
  521.5 64.1 %all-reduce = (f32[512]{0:T(512)}, f32[512]{0:T(512)}) all-reduce(f32[512]{0:T(512)S(1)} %get-tuple-element.13, f32[512]{0:T(512)S(1)} %copy-done.28), channel_id=1, replica_groups=mesh['seq'=16,'head'=8] {'seq','head'}, use_global_device_ids=true, to_apply=%region_7.0 | all-reduce | flops 1024 | bytes 8192 | tf_op jit(solution)/shard_map/psum | solution.py:147
  585.7 3.5 fusion.25
  589.1 70.7 %all-reduce.4.cloned.1.call-done = (f32[512,512]{1,0:T(8,128)}, f32[512,512]{1,0:T(8,128)}, f32[512,2048]{1,0:T(8,128)}, f32[2048,512]{1,0:T(8,128)}) async-done(((f32[512,512]{1,0:T(8,128)}, f32[512,512]{1,0:T(8,128)}, f32[512,2048]{1,0:T(8,128)}, f32[2048,512]{1,0:T(8,128)}), (f32[512,512]{1,0:T(8,128)}, f32[512,512]{1,0:T(8,128)}, f32[512,2048]{1,0:T(8,128)}, ...) | async-done | bytes 10485776 | tf_op jit(solution)/shard_map/psum | solution.py:147
  659.8 2.4 copy.84
  662.2 2.3 copy.85
  664.5 2.1 copy.86
  666.6 1.6 copy-done.9
  668.2 2.1 copy.87
  670.3 1.0 copy-done.1
  (79 shorter events, 1.1 us)
Async XLA Ops:
  7.2 256.2 %copy-start = (bf16[512,2048]{1,0:T(8,128)(2,1)S(1)}, bf16[512,2048]{1,0:T(8,128)(2,1)}, u32[]{:S(2)}) copy-start(bf16[512,2048]{1,0:T(8,128)(2,1)} %param.17) | copy-start | bytes 6291460
  7.2 157.1 %all-gather.2.cloned.1.call-start = ((), (), s32[]{:S(2)}) async-start(), calls=%async_computation.5 | async-start | bytes 17825792 | tf_op jit(solution)/shard_map/all_gather | solution.py:77
  8.1 1.5 copy-start.24
  9.6 0.6 copy-start.22
  49.0 4.1 copy-start.13
  49.0 4.2 copy-start.26
  53.3 156.5 %copy-start.29 = (f32[64]{0:T(128)}, f32[64]{0:T(128)S(1)}, u32[]{:S(2)}) copy-start(f32[64]{0:T(128)S(1)} %reduce_max.15) | copy-start | bytes 772
  53.6 0.6 copy-start.20
  53.7 259.3 %copy-start.21 = (f32[128,64]{1,0:T(8,128)}, f32[128,64]{1,0:T(8,128)S(1)}, u32[]{:S(2)}) copy-start(f32[128,64]{1,0:T(8,128)S(1)} %copy.61) | copy-start | bytes 98308
  54.4 155.4 %copy-start.18 = (f32[128,1024]{1,0:T(8,128)}, f32[128,1024]{1,0:T(8,128)S(1)}, u32[]{:S(2)}) copy-start(f32[128,1024]{1,0:T(8,128)S(1)} %fusion.49) | copy-start | bytes 1572868
  225.7 9.7 %copy-start.30 = (bf16[512]{0:T(512)(128)(2,1)S(1)}, bf16[512]{0:T(512)(128)(2,1)}, u32[]{:S(2)}) copy-start(bf16[512]{0:T(512)(128)(2,1)} %param.16) | copy-start | bytes 3076
  230.1 20.2 %all-to-all-start.1 = ((bf16[8,2,32768]{2,1,0:T(2,128)(2,1)}), bf16[8,2,32768]{2,1,0:T(2,128)(2,1)S(1)}, u32[]{:S(2)}, u32[]{:S(2)}) async-start(bf16[8,2,32768]{2,1,0:T(2,128)(2,1)} %reshape.216), calls=%async_computation.1 | async-start | bytes 2097152 | tf_op jit(solution)/shard_map/all_to_all | solution.py:87
  235.2 221.8 %reduce-scatter.2.cloned.1.call-start = ((), (), s32[]{:S(2)}) async-start(), calls=%async_computation.6 | async-start | bytes 17825792 | tf_op jit(solution)/shard_map/reduce_scatter | solution.py:130
  257.1 4.1 copy-start.8
  263.4 12.4 %copy-start.2 = (f32[16,64,512]{2,1,0:T(8,128)}, f32[16,64,512]{2,1,0:T(8,128)S(1)}, u32[]{:S(2)}) copy-start(f32[16,64,512]{2,1,0:T(8,128)S(1)} %get-tuple-element.24) | copy-start | bytes 6291460
  263.4 4.6 copy-start.15
  263.4 4.6 copy-start.31
  272.6 3.2 copy-start.6
  275.8 1.0 copy-start.11
  276.8 5.5 copy-start.4
  310.6 2.4 copy-start.19
  348.6 3.8 copy-start.3
  348.6 3.8 copy-start.32
  352.4 5.7 copy-start.7
  463.6 5.9 copy-start.16
  463.6 20.8 %all-to-all-start.3 = ((bf16[8,2,32768]{2,1,0:T(2,128)(2,1)}), bf16[8,2,32768]{2,1,0:T(2,128)(2,1)}, u32[]{:S(2)}, u32[]{:S(2)}) async-start(bf16[8,2,32768]{2,1,0:T(2,128)(2,1)} %reshape.220), calls=%async_computation.4 | async-start | bytes 2097152 | tf_op jit(solution)/shard_map/all_to_all | solution.py:138
  469.2 190.6 %all-reduce.4.cloned.1.call-start = ((), (), s32[]{:S(2)}) async-start(), calls=%async_computation.7 | async-start | bytes 20971520 | tf_op jit(solution)/shard_map/psum | solution.py:147
  490.6 3.2 copy-start.23
  490.6 3.2 copy-start.25
  493.9 1.9 copy-start.17
  495.7 1.6 copy-start.12
  497.3 18.5 %copy-start.14 = (bf16[1,64,1024]{2,1,0:T(8,128)(2,1)S(1)}, bf16[1,64,1024]{2,1,0:T(8,128)(2,1)}, u32[]{:S(2)}) copy-start(bf16[1,64,1024]{2,1,0:T(8,128)(2,1)} %param.14) | copy-start | bytes 393220
  497.3 18.5 %copy-start.27 = (s32[128]{0:T(128)S(1)}, s32[128]{0:T(128)}, u32[]{:S(2)}) copy-start(s32[128]{0:T(128)} %param.11) | copy-start | bytes 1540
  517.8 3.8 copy-start.28
  517.8 67.9 %copy-start.5 = (f32[16,64,512]{2,1,0:T(8,128)S(1)}, f32[16,64,512]{2,1,0:T(8,128)}, u32[]{:S(2)}) copy-start(f32[16,64,512]{2,1,0:T(8,128)} %copy-done.4) | copy-start | bytes 6291460
  659.8 4.7 copy-start.10
  664.5 3.7 copy-start.9
  668.2 3.1 copy-start.1
Sparse Core Ops, SparseCore 0:
  53.2 111.0 all-gather.1
  348.7 108.1 reduce-scatter.1
  495.9 163.8 all-reduce.3
where the time goes:
time: 688 us; the launch traced here: 678 us
  waiting for transfers between devices  298 us (43%)
  local copies, waits for them, and re-layouts  151 us (22%)
  blocking collectives  104 us (15%)
  matrix products  90 us (13%)
  between operations  14.6 us (2%)
  starting transfers between devices  11.2 us (2%)
  other arithmetic  9.39 us (1%)
    all_gather x1, waiting for transfers between devices, shards(): every_value = lax.all_gather(head_values, 'seq', axis=1, tiled=True)  110 us
    reduce_scatter x1, waiting for transfers between devices, shards(): lax.psum_scatter(term.reshape(local_rows * lax.axis_size('seq'), bucket_c...  94.3 us
    psum x1, waiting for transfers between devices, shards(): lax.psum((norm_gain_grad, value_weight_grad, out_grad, ffn_gain_grad, up_...  70.7 us
    psum x1, blocking collectives, shards(): lax.psum((norm_gain_grad, value_weight_grad, out_grad, ffn_gain_grad, up_...  64.1 us
    all_gather x1, local copies, waits for them, and re-layouts, shards(): every_value = lax.all_gather(head_values, 'seq', axis=1, tiled=True)  45.5 us
    unnamed x78, local copies, waits for them, and re-layouts  40.9 us
    convert_element_type x1, local copies, waits for them, and re-layouts, shards(): term.reshape(local_rows * lax.axis_size('seq'), bucket_count, head_width)  26 us
    all_to_all x1, blocking collectives, shards(): lax.all_to_all(values, 'head', split_axis=2, concat_axis=0, tiled=True)  21.8 us
  transfers between devices with their start and end apart: 5, of which 5 were waited for; matrix products, arithmetic and copies ran while one was open for 7% of the time, Pallas kernels for 0%

commit v1 on v0

v1 whole, which is shorter than its diff:
```python
import functools
import math

import jax
import jax.numpy as jnp
from jax import lax
from jax.experimental import pallas as pl
from jax.experimental.pallas import tpu as pltpu
from jax.sharding import PartitionSpec as P

EPS = 1e-06
ROOT_HALF = 1.0 / math.sqrt(2.0)
DENSITY = 1.0 / math.sqrt(2.0 * math.pi)
LANES = 128
CHUNK = 32
PER = LANES // CHUNK
BOTH = ("seq", "head")
bf16 = jnp.bfloat16
f32 = jnp.float32


def nt(left, right):
    return lax.dot_general(left, right, (((1,), (1,)), ((), ())), preferred_element_type=f32)


def tn(left, right):
    return lax.dot_general(left, right, (((0,), (0,)), ((), ())), preferred_element_type=f32)


def nn(left, right):
    return jnp.dot(left, right, preferred_element_type=f32)


def lane_groups(rows):
    return lax.broadcasted_iota(jnp.int32, (rows, LANES), 1) // CHUNK


def pick(groups, parts):
    out = parts[PER - 1]
    for l in range(PER - 2, -1, -1):
        out = jnp.where(groups == l, parts[l], out)
    return out


def spread(value, store):
    rows = value.shape[0] // PER
    groups = lane_groups(rows)
    for q in range(value.shape[1] // LANES):
        turned = []
        for r in range(PER):
            piece = value[r * rows : (r + 1) * rows, q * LANES : (q + 1) * LANES]
            turned.append(pltpu.roll(piece, CHUNK * r, 1) if r else piece)
        for k in range(PER):
            store(q * PER + k, pick(groups, [turned[(l - k) % PER] for l in range(PER)]))


def collect(ref, group):
    chunks, rows, _ = ref.shape
    lanes = slice(group * LANES, (group + 1) * LANES)
    groups = lane_groups(rows)
    columns = []
    for q in range(chunks // PER):
        loaded = [ref[q * PER + k, :, lanes].astype(f32) for k in range(PER)]
        parts = []
        for r in range(PER):
            mixed = pick(groups, [loaded[(l - r) % PER] for l in range(PER)])
            parts.append(pltpu.roll(mixed, LANES - CHUNK * r, 1) if r else mixed)
        columns.append(jnp.concatenate(parts, axis=0))
    return jnp.concatenate(columns, axis=1)


def places():
    seq = lax.axis_index("seq")
    head = lax.axis_index("head")
    return seq // 4, seq % 4, head // 2, head % 2


def row_keep(lens_ref, buckets, rows):
    first = lax.axis_index("head") * (lens_ref.shape[0] // lax.axis_size("head"))
    start = lax.axis_index("seq") * rows
    spot = start + lax.broadcasted_iota(jnp.int32, (rows, 1), 0)
    parts = []
    for r in range(buckets):
        length = lens_ref[first + pl.program_id(0) * buckets + r]
        parts.append((spot < length).astype(f32))
    return jnp.concatenate(parts, axis=0)


def gain_row(gain_ref):
    return gain_ref[...].astype(f32).reshape(1, gain_ref.shape[0])


def rms(values):
    scale = lax.rsqrt(jnp.mean(values * values, axis=-1, keepdims=True) + EPS)
    return values * scale, scale


def values_kernel(lens_ref, tok_ref, gain_ref, vw_ref, out_ref):
    per, rows, width = tok_ref.shape
    tok = tok_ref[...].reshape(per * rows, width).astype(f32)
    normed, _ = rms(tok)
    hidden = (normed * gain_row(gain_ref)).astype(bf16)
    val = nn(hidden, vw_ref[...]) * row_keep(lens_ref, per, rows)

    def store(chunk, block):
        out_ref[chunk] = block.astype(bf16)

    spread(val, store)


def lane_lengths(lens_ref, lanes):
    _, y, _, _ = places()
    group = lanes // CHUNK
    first = lax.axis_index("head") * group
    lane = lax.broadcasted_iota(jnp.int32, (1, lanes), 1) // CHUNK
    lens = jnp.zeros((1, lanes), jnp.int32)
    for n in range(group):
        m, l = divmod(n, PER)
        lens = jnp.where(lane == n, lens_ref[first + m * PER + (l - y + PER) % PER], lens)
    return lens


def mix_kernel(lens_ref, *refs):
    count = len(refs) - 12
    pieces = refs[:count]
    held_ref, exp_out, inv_out, mix_out = refs[count : count + 4]
    landed, held, keep, expo, inverse, mixed, sems, out_sems = refs[count + 4 :]
    span, lanes = held.shape
    _, y, z, c = places()
    half = pieces[0].shape[0] // 2
    copies = []
    for n, piece in enumerate(pieces):
        for k in range(2):
            spot = pl.multiple_of((y + k) % 2 * half, half)
            copies.append(
                pltpu.make_async_copy(
                    piece.at[pl.ds(k * half, half), :],
                    landed.at[n, pl.ds(spot, half), :],
                    sems.at[n, k],
                )
            )
    held_copy = pltpu.make_async_copy(held_ref, held, sems.at[count, 0])
    copies[0].start()
    copies[1].start()
    held_copy.start()
    for copy in copies[2:]:
        copy.start()
    lens = lane_lengths(lens_ref, lanes)
    place = lax.broadcasted_iota(jnp.int32, (span, lanes), 0)
    keep[...] = (place < lens).astype(f32).astype(bf16)
    out_copies = []
    for n in range(count):
        copies[2 * n].wait()
        copies[2 * n + 1].wait()
        core = c if n < 4 else 1 - c
        start = pl.multiple_of((((z - n % 4 + 4) % 4) * 4 + core * 2) * half, 2 * half)
        logits = landed[n].astype(f32)
        part = jnp.exp(logits - jnp.max(logits, axis=-1, keepdims=True)).astype(bf16)
        expo[n] = part
        here = start + lax.broadcasted_iota(jnp.int32, (2 * half, lanes), 0)
        inverted = jnp.where(here < lens, 1.0 / nn(part, keep[...]), 0.0)
        inverse[n] = inverted
        if n == 0:
            held_copy.wait()
        mixed[n] = (nn(part, held[...]) * inverted).astype(bf16)
        for k, (source, target) in enumerate(
            ((mixed, mix_out), (expo, exp_out), (inverse, inv_out))
        ):
            copy = pltpu.make_async_copy(
                source.at[n], target.at[pl.ds(start, 2 * half), :], out_sems.at[n, k]
            )
            copy.start()
            out_copies.append(copy)
    for copy in out_copies:
        copy.wait()


def unmix_kernel(exp_ref, gm_ref, inv_ref, mixed_ref, out_ref, g_ref, r_ref, acc_ref):
    scaled = gm_ref[...].astype(f32) * inv_ref[...]
    low = scaled.astype(bf16)
    g_ref[...] = low
    r_ref[...] = (scaled * mixed_ref[...].astype(f32)).astype(bf16)
    part = tn(exp_ref[...], low)
    step = pl.program_id(0)

    @pl.when(step == 0)
    def _():
        acc_ref[...] = part

    @pl.when(step > 0)
    def _():
        acc_ref[...] += part

    @pl.when(step == pl.num_programs(0) - 1)
    def _():
        out_ref[...] = acc_ref[...].astype(bf16)


def scores_kernel(lens_ref, g_ref, r_ref, val_ref, out_ref, keep_ref):
    span, lanes = val_ref.shape

    @pl.when(pl.program_id(0) == 0)
    def _():
        place = lax.broadcasted_iota(jnp.int32, (span, lanes), 0)
        keep_ref[...] = (place < lane_lengths(lens_ref, lanes)).astype(f32).astype(bf16)

    out = nt(g_ref[...], val_ref[...]) - nt(r_ref[...], keep_ref[...])
    out_ref[...] = out.astype(bf16)


def ffn_kernel(
    lens_ref,
    tok_ref,
    cot_ref,
    mix_ref,
    ow_ref,
    gain_ref,
    up_ref,
    down_ref,
    out_ref,
    gr_ref,
    gm_ref,
    grads_ref,
    down_acc,
    up_acc,
    ow_acc,
):
    per, rows, width = tok_ref.shape
    n = per * rows
    ff = up_ref.shape[1]
    step = up_acc.shape[2]

    @pl.when(pl.program_id(0) == 0)
    def _():
        down_acc[...] = jnp.zeros_like(down_acc)
        up_acc[...] = jnp.zeros_like(up_acc)
        ow_acc[...] = jnp.zeros_like(ow_acc)

    keep = row_keep(lens_ref, per, rows)
    tok = tok_ref[...].reshape(n, width).astype(f32)
    grad_low = (cot_ref[...].reshape(n, width).astype(f32) * keep).astype(bf16)
    mixed = jnp.concatenate(
        [collect(mix_ref, g) for g in range(per // PER)], axis=0
    ).astype(bf16)
    resid = tok + nn(mixed, ow_ref[...])
    normed, scale = rms(resid)
    gain = gain_row(gain_ref)
    hidden = (normed * gain).astype(bf16)
    ffn = jnp.zeros((n, width), f32)
    grad_hidden = jnp.zeros((n, width), f32)
    for q in range(ff // step):
        cut = slice(q * step, (q + 1) * step)
        up = up_ref[:, cut]
        down = down_ref[cut, :]
        pre = nn(hidden, up)
        cdf = 0.5 * (1.0 + lax.erf(pre * ROOT_HALF))
        slope = cdf + pre * jnp.exp(-0.5 * pre * pre) * DENSITY
        act = (pre * cdf).astype(bf16)
        ffn = ffn + nn(act, down)
        grad_pre = (nt(grad_low, down) * slope).astype(bf16)
        grad_hidden = grad_hidden + nt(grad_pre, up)
        down_acc[cut, :] += tn(act, grad_low)
        up_acc[q] += tn(hidden, grad_pre)
    out_ref[...] = ((resid + ffn) * keep).astype(bf16).reshape(per, rows, width)
    weighted = grad_hidden * gain
    back = scale * (weighted - normed * jnp.mean(weighted * normed, axis=-1, keepdims=True))
    grad_resid = grad_low.astype(f32) + back
    gr_ref[...] = grad_resid
    grad_att = grad_resid.astype(bf16)
    ow_acc[...] += tn(mixed, grad_att)
    grad_mixed = nt(grad_att, ow_ref[...]) * keep
    size = PER * rows
    for g in range(per // PER):

        def store(chunk, block, g=g):
            gm_ref[chunk, :, g * LANES : (g + 1) * LANES] = block.astype(bf16)

        spread(grad_mixed[g * size : (g + 1) * size], store)

    @pl.when(pl.program_id(0) == pl.num_programs(0) - 1)
    def _():
        half = width // 2
        for k in range(2):
            lanes = slice(k * half, (k + 1) * half)
            grads_ref[k * ff : (k + 1) * ff, :] = down_acc[:, lanes].astype(bf16)
            for q in range(ff // step):
                first = 2 * ff + (2 * q + k) * width
                grads_ref[first : first + width, :] = up_acc[q][:, lanes].astype(bf16)
            first = 4 * ff + k * width
            grads_ref[first : first + width, :] = ow_acc[:, lanes].astype(bf16)


def value_grad_kernel(lens_ref, tok_ref, vg_ref, gain_ref, vgrad_ref, part_ref, acc_ref):
    per, rows, width = tok_ref.shape
    tok = tok_ref[...].reshape(per * rows, width).astype(f32)
    normed, _ = rms(tok)
    hidden = (normed * gain_row(gain_ref)).astype(bf16)
    vgrad = (collect(vg_ref, 0) * row_keep(lens_ref, per, rows)).astype(bf16)
    vgrad_ref[...] = vgrad

    @pl.when(pl.program_id(0) == 0)
    def _():
        acc_ref[...] = jnp.zeros_like(acc_ref)

    acc_ref[...] += tn(hidden, vgrad)

    @pl.when(pl.program_id(0) == pl.num_programs(0) - 1)
    def _():
        _, tall, wide = part_ref.shape
        for i in range(width // tall):
            for j in range(width // wide):
                part_ref[i * (width // wide) + j] = acc_ref[
                    i * tall : (i + 1) * tall, j * wide : (j + 1) * wide
                ].astype(bf16)


def input_grad_kernel(tok_ref, vgrad_ref, gr_ref, gain_ref, vw_ref, out_ref):
    per, rows, width = tok_ref.shape
    tok = tok_ref[...].reshape(per * rows, width).astype(f32)
    normed, scale = rms(tok)
    weighted = nt(vgrad_ref[...], vw_ref[...]) * gain_row(gain_ref)
    back = scale * (weighted - normed * jnp.mean(weighted * normed, axis=-1, keepdims=True))
    out_ref[...] = (gr_ref[...] + back).reshape(per, rows, width)


def sum_spread_kernel(in_ref, out_ref):
    total = jnp.sum(in_ref[...].astype(f32), axis=0)
    out_ref[...] = jnp.broadcast_to(total[None], out_ref.shape).astype(bf16)


def row_total(product):
    folded = sum(
        product[:, n * LANES : (n + 1) * LANES] for n in range(product.shape[1] // LANES)
    )
    return jnp.sum(folded.T, axis=0, keepdims=True)


def finish_ffn_kernel(
    down_one,
    down_two,
    up_in,
    ow_one,
    ow_two,
    up_ref,
    gain_ref,
    down_out,
    up_out,
    ow_out,
    gain_out,
    acc_ref,
):
    q = pl.program_id(0)
    half = down_one.shape[1]
    width = up_out.shape[0]
    down_out[:, :half] = down_one[...].astype(f32)
    down_out[:, half:] = down_two[...].astype(f32)
    up_out[:, :half] = up_in[:width, :].astype(f32)
    up_out[:, half:] = up_in[width:, :].astype(f32)
    product = up_ref[...].astype(f32) * up_out[...]

    @pl.when(q == 0)
    def _():
        acc_ref[...] = product
        ow_out[:, :half] = ow_one[...].astype(f32)
        ow_out[:, half:] = ow_two[...].astype(f32)

    @pl.when(q > 0)
    def _():
        acc_ref[...] += product

    @pl.when(q == pl.num_programs(0) - 1)
    def _():
        gain_out[...] = row_total(acc_ref[...]) / gain_row(gain_ref)


def finish_value_kernel(in_ref, vw_ref, gain_ref, out_ref, gain_out):
    count, tall, wide = in_ref.shape
    across = out_ref.shape[1] // wide
    for n in range(count):
        i, j = divmod(n, across)
        out_ref[i * tall : (i + 1) * tall, j * wide : (j + 1) * wide] = in_ref[n].astype(f32)
    gain_out[...] = row_total(vw_ref[...].astype(f32) * out_ref[...]) / gain_row(gain_ref)


def params():
    return pltpu.CompilerParams(vmem_limit_bytes=58 * 1024 * 1024)


def cost(flops, size):
    return pl.CostEstimate(flops=int(flops), bytes_accessed=int(size), transcendentals=0)


def whole(*shape):
    return pl.BlockSpec(shape, lambda *_: (0,) * len(shape))


def once(*shape):
    return pl.BlockSpec(shape, lambda *_: (0,) * len(shape), pipeline_mode=pl.Buffered(1))


def shaped(dtype, *shape):
    return pltpu.HBM(shape, dtype)


def stay(*arrays):
    return [pltpu.with_memory_space_constraint(array, pltpu.HBM) for array in arrays]


def flat(x, y, z, c):
    return ((x % 4) * 4 + y % 4) * 8 + (z % 4) * 2 + c % 2


def devices():
    for i in range(128):
        s, h = divmod(i, 8)
        yield i, s // 4, s % 4, h // 2, h % 2


def shift(array, x=0, y=0, z=0, c=0):
    pairs = [(i, flat(a + x, b + y, d + z, e + c)) for i, a, b, d, e in devices()]
    return lax.ppermute(array, BOTH, pairs)


def flip(array, y=0, c=0):
    pairs = [(i, flat(a, b ^ y, d, e ^ c)) for i, a, b, d, e in devices()]
    return lax.ppermute(array, BOTH, pairs)


def to_plane(array, odd=0, back=False):
    pairs = [(i, flat(d, 2 * e + ((b & 1) ^ odd), a, b >> 1)) for i, a, b, d, e in devices()]
    if back:
        pairs = [(j, i) for i, j in pairs]
    return lax.ppermute(array, BOTH, pairs)


def swap_seq(array):
    return lax.all_to_all(array, "seq", 0, 0, tiled=True)


def swap_all(array):
    return lax.all_to_all(array, BOTH, 0, 0, tiled=True)


def after(array, *others):
    return lax.optimization_barrier((array,) + others)[0]


def at(array, index):
    return lax.dynamic_index_in_dim(array, index, 0, keepdims=False)


def shards(
    tokens,
    lengths,
    norm_gain,
    value_weight,
    synth_logits,
    out_weight,
    ffn_gain,
    up_weight,
    down_weight,
    cotangent,
):
    group, rows, width = tokens.shape
    span = synth_logits.shape[2]
    ff = up_weight.shape[1]
    blocks = span // rows
    total_rows = group * rows
    steps = group // PER
    tile = PER * rows
    _, y, z, c = places()

    def tok_spec(n):
        return pl.BlockSpec((n, rows, width), lambda m, *_: (m, 0, 0))

    def move_spec(n):
        return pl.BlockSpec((blocks, rows, n // PER * LANES), lambda m, *_: (0, 0, m))

    def row_spec(n, columns):
        return pl.BlockSpec((n, columns), lambda m, *_: (m, 0))

    def call(kernel, grid, ins, outs, shapes, flops, size, scratch=(), prefetch=0):
        return pl.pallas_call(
            kernel,
            grid_spec=pltpu.PrefetchScalarGridSpec(
                num_scalar_prefetch=prefetch,
                grid=grid,
                in_specs=ins,
                out_specs=outs,
                scratch_shapes=scratch,
            ),
            out_shape=shapes,
            compiler_params=params(),
            cost_estimate=cost(flops, size),
        )

    with jax.named_scope("logits"):
        block = synth_logits.reshape(rows, span)
        halves = [to_plane(block), to_plane(block, odd=1)]

    with jax.named_scope("values"):
        sent_values = call(
            values_kernel,
            (steps,),
            [tok_spec(PER), whole(width), whole(width, width)],
            move_spec(PER),
            shaped(bf16, blocks, rows, width),
            2 * total_rows * width * width,
            3e6,
            prefetch=1,
        )(lengths, *stay(tokens, norm_gain, value_weight))
        halves = lax.optimization_barrier((*halves, sent_values))
        sent_values = halves[2]
        held = swap_seq(sent_values).reshape(span, width)

    with jax.named_scope("logits"):
        pair = jnp.concatenate(halves[:2])
        pieces = [pair] + [shift(pair, z=step) for step in (1, 2, 3)]
        pieces = pieces + [flip(piece, c=1) for piece in pieces]

    quarter = span // 4
    with jax.named_scope("mix"):
        anywhere = pl.BlockSpec(memory_space=pl.ANY)
        expo, inverse, mixed_held = call(
            mix_kernel,
            (1,),
            [anywhere] * 9,
            [anywhere] * 3,
            [shaped(bf16, span, span), shaped(f32, span, width), shaped(bf16, span, width)],
            4 * span * span * width,
            8e6,
            scratch=[
                pltpu.VMEM((8, 2 * rows, span), bf16),
                pltpu.VMEM((span, width), bf16),
                pltpu.VMEM((span, width), bf16),
                pltpu.VMEM((8, 2 * rows, span), bf16),
                pltpu.VMEM((8, 2 * rows, width), f32),
                pltpu.VMEM((8, 2 * rows, width), bf16),
                pltpu.SemaphoreType.DMA((9, 2)),
                pltpu.SemaphoreType.DMA((8, 3)),
            ],
            prefetch=1,
        )(lengths, *stay(*pieces, held))
        got_mixed = swap_seq(mixed_held.reshape(blocks, rows, width))

    grad_rows = 4 * ff + 2 * width
    with jax.named_scope("ffn"):
        output, grad_resid, sent_grad, ffn_part = call(
            ffn_kernel,
            (steps // 2,),
            [
                tok_spec(2 * PER),
                tok_spec(2 * PER),
                move_spec(2 * PER),
                once(width, width),
                once(width),
                once(width, ff),
                once(ff, width),
            ],
            [
                tok_spec(2 * PER),
                row_spec(2 * tile, width),
                move_spec(2 * PER),
                once(grad_rows, width // 2),
            ],
            [
                shaped(bf16, group, rows, width),
                shaped(f32, total_rows, width),
                shaped(bf16, blocks, rows, width),
                shaped(bf16, grad_rows, width // 2),
            ],
            2 * total_rows * width * (6 * ff + 3 * width),
            2e7,
            scratch=[
                pltpu.VMEM((ff, width), f32),
                pltpu.VMEM((ff // width, width, width), f32),
                pltpu.VMEM((width, width), f32),
            ],
            prefetch=1,
        )(
            lengths,
            *stay(tokens, cotangent, got_mixed, out_weight, ffn_gain, up_weight, down_weight),
        )
        got_grad = swap_seq(sent_grad).reshape(span, width)

    with jax.named_scope("ffn_sum"):
        ffn_sum = lax.psum_scatter(ffn_part, "head", scatter_dimension=0, tiled=True)

    with jax.named_scope("unmix"):
        held_grad, g_scaled, r_scaled = call(
            unmix_kernel,
            (4,),
            [row_spec(quarter, span)] + [row_spec(quarter, width)] * 3,
            [whole(span, width), row_spec(quarter, width), row_spec(quarter, width)],
            [shaped(bf16, span, width)] * 3,
            2 * span * span * width,
            9e6,
            scratch=[pltpu.VMEM((span, width), f32)],
        )(*stay(expo, got_grad, inverse, mixed_held))
        got_values = swap_seq(held_grad.reshape(blocks, rows, width))

    with jax.named_scope("scores"):
        scores = call(
            scores_kernel,
            (4,),
            [row_spec(quarter, width), row_spec(quarter, width), whole(span, width)],
            row_spec(quarter, span),
            shaped(bf16, span, span),
            4 * span * span * width,
            8e6,
            scratch=[pltpu.VMEM((span, width), bf16)],
            prefetch=1,
        )(lengths, *stay(g_scaled, r_scaled, held))
        ffn_sum, scores, got_values = lax.optimization_barrier((ffn_sum, scores, got_values))
        scores = lax.psum_scatter(scores, "head", scatter_dimension=0, tiled=True)

    with jax.named_scope("ffn_sum"):
        piece = grad_rows // 8 // blocks
        ffn_sum = swap_seq(ffn_sum.reshape(blocks, piece, width // 2))
        ffn_sum = call(
            sum_spread_kernel,
            (1,),
            [whole(blocks, piece, width // 2)],
            whole(blocks, piece, width // 2),
            shaped(bf16, blocks, piece, width // 2),
            1e6,
            1e6,
        )(ffn_sum)
        ffn_sum = swap_seq(ffn_sum).reshape(grad_rows // 8, width // 2)
        ffn_sum = lax.all_gather(ffn_sum, "head", axis=0, tiled=True)

    with jax.named_scope("value_grad"):
        value_grad, value_part = call(
            value_grad_kernel,
            (steps,),
            [tok_spec(PER), move_spec(PER), whole(width)],
            [row_spec(tile, width), whole(128, 16, 128)],
            [shaped(bf16, total_rows, width), shaped(bf16, 128, 16, 128)],
            2 * total_rows * width * width,
            4e6,
            scratch=[pltpu.VMEM((width, width), f32)],
            prefetch=1,
        )(lengths, *stay(tokens), got_values, *stay(norm_gain))
        spread_all = call(
            sum_spread_kernel,
            (1,),
            [whole(128, 16, 128)],
            whole(128, 16, 128),
            shaped(bf16, 128, 16, 128),
            1e6,
            1e6,
        )
        value_sum = swap_all(spread_all(swap_all(value_part)))

    with jax.named_scope("input_grad"):
        input_grad = call(
            input_grad_kernel,
            (steps,),
            [
                tok_spec(PER),
                row_spec(tile, width),
                row_spec(tile, width),
                whole(width),
                whole(width, width),
            ],
            tok_spec(PER),
            shaped(f32, group, rows, width),
            2 * total_rows * width * width,
            7e6,
        )(*stay(tokens), value_grad, *stay(grad_resid, norm_gain, value_weight))

    with jax.named_scope("ffn_sum"):
        count = ff // width
        half_spec = pl.BlockSpec((width, width // 2), lambda q: (q, 0))
        down_grad, up_grad, out_grad, ffn_gain_grad = call(
            finish_ffn_kernel,
            (count,),
            [
                half_spec,
                pl.BlockSpec((width, width // 2), lambda q: (count + q, 0)),
                pl.BlockSpec((2 * width, width // 2), lambda q: (count + q, 0)),
                pl.BlockSpec((width, width // 2), lambda q: (4 * count, 0)),
                pl.BlockSpec((width, width // 2), lambda q: (4 * count + 1, 0)),
                pl.BlockSpec((width, width), lambda q: (0, q)),
                whole(width),
            ],
            [
                pl.BlockSpec((width, width), lambda q: (q, 0)),
                pl.BlockSpec((width, width), lambda q: (0, q)),
                whole(width, width),
                whole(1, width),
            ],
            [
                shaped(f32, ff, width),
                shaped(f32, width, ff),
                shaped(f32, width, width),
                shaped(f32, 1, width),
            ],
            4e6,
            13e6,
            scratch=[pltpu.VMEM((width, width), f32)],
        )(*stay(*[ffn_sum] * 5, up_weight, ffn_gain))

    with jax.named_scope("value_sum"):
        value_weight_grad, norm_gain_grad = call(
            finish_value_kernel,
            (1,),
            [whole(128, 16, 128), whole(width, width), whole(width)],
            [whole(width, width), whole(1, width)],
            [shaped(f32, width, width), shaped(f32, 1, width)],
            4e6,
            2e6,
        )(value_sum, *stay(value_weight, norm_gain))

    with jax.named_scope("logits_grad"):
        parts = scores.reshape(2, rows, span)
        low = y % 2
        part = at(parts, low).astype(f32) + flip(at(parts, 1 - low), y=1).astype(f32)
        part = to_plane(part.astype(bf16), back=True).astype(f32)
        logits = synth_logits.reshape(rows, span).astype(f32)
        exact = jnp.exp(logits - jnp.max(logits, axis=-1, keepdims=True))
        logits_grad = (part * exact).reshape(1, rows, span)
    return (
        output,
        input_grad,
        norm_gain_grad.reshape(width),
        value_weight_grad,
        logits_grad,
        out_grad,
        ffn_gain_grad.reshape(width),
        up_grad,
        down_grad,
    )


def solution(mesh):
    token_spec = P("head", "seq", None)
    placed = (
        token_spec,
        P(),
        P(),
        P(),
        token_spec,
        P(),
        P(),
        P(),
        P(),
        token_spec,
    )
    return jax.shard_map(
        shards,
        mesh=mesh,
        in_specs=placed,
        out_specs=(token_spec, token_spec, P(), P(), token_spec, P(), P(), P(), P()),
        check_vma=False,
    )
```

time: 688 us -> 263 us (0.38)
  waiting for transfers between devices: 298 us -> 38.4 us
  local copies, waits for them, and re-layouts: 151 us -> 6.12 us
  matrix products: 90 us -> 0 us
  Pallas kernels: 0 us -> 75.9 us
  starting transfers between devices: 11.2 us -> 54.2 us
  blocking collectives: 104 us -> 69 us
  other arithmetic: 9.39 us -> 1.89 us
    all_gather x1, waiting for transfers between devices: 110 us -> 0.01 us  [shards(): ffn_sum = lax.all_gather(ffn_sum, 'head', axis=0, tiled=True)]
    reduce_scatter x1 -> x2, waiting for transfers between devices: 94.3 us -> 0.02 us  [the longest x1 0.02 us: shards(): scores = lax.psum_scatter(scores, 'head', scatter_dimension=0, tiled=True)]
    dot_general x17 -> x0, matrix products: 90 us -> none  [the longest x1 17.5 us: shards(): jnp.einsum('bihd,bjhd->bhij', grad_heads, segment_heads, preferred_elemen...]
    pallas_call x0 -> x11, Pallas kernels: none -> 75.9 us  [the longest x1 25.5 us: shards(): call(ffn_kernel, (steps // 2,), [tok_spec(2 * PER), tok_spec(2 * PER), mo...]
    psum x1 -> x0, waiting for transfers between devices: 70.7 us -> none  [shards(): lax.psum((norm_gain_grad, value_weight_grad, out_grad, ffn_gain_grad, up_...]
    psum x1 -> x0, blocking collectives: 64.1 us -> none  [shards(): lax.psum((norm_gain_grad, value_weight_grad, out_grad, ffn_gain_grad, up_...]
    all_gather x1 -> x0, local copies, waits for them, and re-layouts: 45.5 us -> none  [shards(): every_value = lax.all_gather(head_values, 'seq', axis=1, tiled=True)]
    unnamed x78 -> x31, local copies, waits for them, and re-layouts: 40.9 us -> 5.18 us
  transfers between devices with their start and end apart: 5 -> 18, of which waited for: 5 -> 7; matrix products, arithmetic and copies ran while one was open for 7% -> 1% of each run, Pallas kernels for 0% -> 14%
where the time goes in v1:
time: 263 us; the launch traced here: 260 us
  Pallas kernels  75.9 us (29%)
  blocking collectives  69 us (26%)
  starting transfers between devices  54.2 us (21%)
  waiting for transfers between devices  38.4 us (15%)
  between operations  14 us (5%)
  local copies, waits for them, and re-layouts  6.12 us (2%)
    all_to_all x4, blocking collectives, swap_seq(): return lax.all_to_all(array, 'seq', 0, 0, tiled=True)  69 us
    pallas_call x1, Pallas kernels, shards(): call(ffn_kernel, (steps // 2,), [tok_spec(2 * PER), tok_spec(2 * PER), mo...  25.5 us
    all_to_all x2, starting transfers between devices, swap_seq(): return lax.all_to_all(array, 'seq', 0, 0, tiled=True)  16.3 us
    all_to_all x2, waiting for transfers between devices, swap_all(): return lax.all_to_all(array, BOTH, 0, 0, tiled=True)  13.8 us
    all_to_all x2, starting transfers between devices, swap_all(): return lax.all_to_all(array, BOTH, 0, 0, tiled=True)  13 us
    ppermute x3, starting transfers between devices, to_plane(): return lax.ppermute(array, BOTH, pairs)  12.2 us
    ppermute x5, starting transfers between devices, flip(): return lax.ppermute(array, BOTH, pairs)  9.14 us
    ppermute x5, waiting for transfers between devices, flip(): return lax.ppermute(array, BOTH, pairs)  8.25 us
  transfers between devices with their start and end apart: 18, of which 7 were waited for; matrix products, arithmetic and copies ran while one was open for 1% of the time, Pallas kernels for 14%

profile of v1, /device:TPU:1, one launch (start us, length us, event | category | flops | bytes accessed | tf_op | source)
XLA Modules:
  0.0 259.6 jit_solution(5226040767103545228)
XLA Ops:
  7.2 4.2 %collective-permute-start.1 = (bf16[64,1024]{1,0:T(8,128)(2,1)}, bf16[64,1024]{1,0:T(8,128)(2,1)S(1)}, u32[]{:S(2)}, u32[]{:S(2)}) collective-permute-start(bf16[64,1024]{1,0:T(8,128)(2,1)} %bitcast.25), channel_id=1, source_target_pairs={{0,8},{1,24},{2,40},{3,56},{4,72},{5,88},{6,104},{7,120},{8,0},{9,... | collective-permute-start | bytes 393224 | tf_op jit(solution)/shard_map/logits/ppermute | solution.py:433
  11.4 2.1 collective-permute-start
  13.5 5.2 %values.1 = bf16[16,64,512]{2,1,0:T(8,128)(2,1)} custom-call(s32[128]{0:T(128)} %lens_ref.9, bf16[16,64,512]{2,1,0:T(8,128)(2,1)} %tok_ref.7, bf16[512]{0:T(512)(128)(2,1)} %gain_ref.10, bf16[512,512]{1,0:T(8,128)(2,1)} %vw_ref.5), custom_call_target="tpu_custom_call" | custom-call | flops 536870912 | bytes 3000000 | tf_op jit(solution)/shard_map/values/pallas_call | solution.py:502
  18.7 0.0 collective-permute-done.1
  18.7 1.5 collective-permute-done
  20.2 12.6 %all-to-all-start = ((bf16[16,64,512]{2,1,0:T(8,128)(2,1)}), bf16[16,64,512]{2,1,0:T(8,128)(2,1)S(1)}, u32[]{:S(2)}, u32[]{:S(2)}) async-start(bf16[16,64,512]{2,1,0:T(8,128)(2,1)} %values.1), calls=%async_computation | async-start | bytes 2097152 | tf_op jit(solution)/shard_map/values/all_to_all | solution.py:437
  32.8 0.0 reduce-scatter.3.cloned.1.call-start
  32.9 0.0 copy-start.7
  32.9 2.8 %collective-permute-start.4 = (bf16[128,1024]{1,0:T(8,128)(2,1)S(1)}, bf16[128,1024]{1,0:T(8,128)(2,1)S(1)}, u32[]{:S(2)}, u32[]{:S(2)}) collective-permute-start(bf16[128,1024]{1,0:T(8,128)(2,1)S(1)} %constant_dynamic-update-slice_fusion.refs_0_), channel_id=1, source_target_pairs={{0,6},{1,7},{2,0},{3,1},{4,2},{5,3},{6,4},{7,5},{8,14},{9,15},{10,... | collective-permute-start | bytes 786440 | tf_op jit(solution)/shard_map/logits/ppermute | solution.py:421
  35.7 0.0 collective-permute-start.3
  35.7 0.7 collective-permute-start.2
  36.4 1.9 collective-permute-start.5
  38.3 4.8 %collective-permute-done.4.refs_3_ = bf16[128,1024]{1,0:T(8,128)(2,1)S(1)} collective-permute-done((bf16[128,1024]{1,0:T(8,128)(2,1)S(1)}, bf16[128,1024]{1,0:T(8,128)(2,1)S(1)}, u32[]{:S(2)}, u32[]{:S(2)}) %collective-permute-start.4) | collective-permute-done | bytes 262176 | tf_op jit(solution)/shard_map/logits/ppermute | solution.py:421
  43.1 4.7 %collective-permute-start.8 = (bf16[128,1024]{1,0:T(8,128)(2,1)S(1)}, bf16[128,1024]{1,0:T(8,128)(2,1)S(1)}, u32[]{:S(2)}, u32[]{:S(2)}) collective-permute-start(bf16[128,1024]{1,0:T(8,128)(2,1)S(1)} %collective-permute-done.4.refs_3_), channel_id=1, source_target_pairs={{0,1},{1,0},{2,3},{3,2},{4,5},{5,4},{6,7},{7,6},{8,9},{9,8},{10,11... | collective-permute-start | bytes 786440 | tf_op jit(solution)/shard_map/logits/ppermute | solution.py:426
  47.8 0.0 collective-permute-done.3.refs_2_
  47.9 0.1 collective-permute-start.7
  47.9 2.5 collective-permute-done.2.refs_1_
  50.4 0.8 collective-permute-start.6
  51.3 0.0 collective-permute-done.5.refs_4_
  51.3 0.0 collective-permute-done.8.refs_7_
  51.3 0.0 collective-permute-done.7.refs_6_
  51.3 1.1 collective-permute-done.6.refs_5_
  52.4 0.0 all-to-all-done
  52.4 0.0 copy-done.8
  52.5 0.6 copy-done.14
  53.1 0.3 copy-done.3
  53.5 7.3 %mix.1 = (bf16[1024,1024]{1,0:T(8,128)(2,1)}, f32[1024,512]{1,0:T(8,128)}, bf16[1024,512]{1,0:T(8,128)(2,1)}) custom-call(s32[128]{0:T(128)} %lens_ref.9, bf16[128,1024]{1,0:T(8,128)(2,1)} %copy-done.7, bf16[128,1024]{1,0:T(8,128)(2,1)} %copy-done.10, bf16[128,1024]{1,0:T(8,128)(2,1)} %copy-done.9, bf16[128,1024]{1,0:T(8,128)(2,1)} %copy-done.8, ...), custom_call_target="tpu_custom_call" | custom-call | flops 2147483648 | bytes 8000000 | tf_op jit(solution)/shard_map/mix/pallas_call | solution.py:524
  60.8 22.7 %all_to_all.40.mix_ref = bf16[16,64,512]{2,1,0:T(8,128)(2,1)} all-to-all(bf16[16,64,512]{2,1,0:T(8,128)(2,1)} %bitcast.18), channel_id=1, replica_groups=mesh['seq'=16,'head'=8] {'seq'}, dimensions={0} | all-to-all | bytes 2097152 | tf_op jit(solution)/shard_map/mix/all_to_all | solution.py:437
  83.5 25.5 %ffn.1 = (bf16[16,64,512]{2,1,0:T(8,128)(2,1)}, f32[1024,512]{1,0:T(8,128)}, bf16[16,64,512]{2,1,0:T(8,128)(2,1)}, bf16[9216,256]{1,0:T(8,128)(2,1)}) custom-call(s32[128]{0:T(128)} %lens_ref.9, bf16[16,64,512]{2,1,0:T(8,128)(2,1)} %tok_ref.7, bf16[16,64,512]{2,1,0:T(8,128)(2,1)} %cot_ref.1, bf16[16,64,512]{2,1,0:T(8,128)(2,1)} %all_to_all.40.mix_ref, ...), custom_call_target="tpu_custom_call" | custom-call | flops 14495514624 | bytes 20000000 | tf_op jit(solution)/shard_map/ffn/pallas_call | solution.py:548
  109.0 0.0 reduce-scatter.3.cloned.1.call-update
  109.0 1.2 copy-done.4
  110.2 18.5 %all_to_all.41 = bf16[16,64,512]{2,1,0:T(8,128)(2,1)} all-to-all(bf16[16,64,512]{2,1,0:T(8,128)(2,1)S(1)} %copy-done.4), channel_id=1, replica_groups=mesh['seq'=16,'head'=8] {'seq'}, dimensions={0} | all-to-all | bytes 2097152 | tf_op jit(solution)/shard_map/ffn/all_to_all | solution.py:437
  128.7 6.5 %unmix.1 = (bf16[1024,512]{1,0:T(8,128)(2,1)}, bf16[1024,512]{1,0:T(8,128)(2,1)}, bf16[1024,512]{1,0:T(8,128)(2,1)}) custom-call(bf16[1024,1024]{1,0:T(8,128)(2,1)} %get-tuple-element.39.exp_ref, bf16[1024,512]{1,0:T(8,128)(2,1)} %bitcast.19, f32[1024,512]{1,0:T(8,128)} %get-tuple-element.41.inv_ref, bf16[1024,512]{1,0:T(8,128)(2,1)} %get-tuple-element.36.mixed_ref), custom_call_target="tpu_custom_call" | custom-call | flops 1073741824 | bytes 9000000 | tf_op jit(solution)/shard_map/unmix/pallas_call | solution.py:590
  135.1 3.7 %all-to-all-start.3 = ((bf16[16,64,512]{2,1,0:T(8,128)(2,1)}), bf16[16,64,512]{2,1,0:T(8,128)(2,1)S(1)}, u32[]{:S(2)}, u32[]{:S(2)}) async-start(bf16[16,64,512]{2,1,0:T(8,128)(2,1)} %bitcast.23), calls=%async_computation.4 | async-start | bytes 2097152 | tf_op jit(solution)/shard_map/unmix/all_to_all | solution.py:437
  138.8 0.0 reduce-scatter.5.cloned.1.call-start
  138.9 6.6 %scores.1 = bf16[1024,1024]{1,0:T(8,128)(2,1)} custom-call(s32[128]{0:T(128)} %lens_ref.9, bf16[1024,512]{1,0:T(8,128)(2,1)} %get-tuple-element.42.g_ref, bf16[1024,512]{1,0:T(8,128)(2,1)} %get-tuple-element.43.r_ref, bf16[1024,512]{1,0:T(8,128)(2,1)} %bitcast.22), custom_call_target="tpu_custom_call" | custom-call | flops 2147483648 | bytes 8000000 | tf_op jit(solution)/shard_map/scores/pallas_call | solution.py:603
  145.5 7.5 %all-to-all-done.3.vg_ref = bf16[16,64,512]{2,1,0:T(8,128)(2,1)S(1)} async-done(((bf16[16,64,512]{2,1,0:T(8,128)(2,1)}), bf16[16,64,512]{2,1,0:T(8,128)(2,1)S(1)}, u32[]{:S(2)}, u32[]{:S(2)}) %all-to-all-start.3) | async-done | bytes 1048608 | tf_op jit(solution)/shard_map/unmix/all_to_all | solution.py:437
  153.0 0.0 reduce-scatter.5.cloned.1.call-update
  153.0 0.0 all-gather.2.cloned.1.call-start
  153.1 1.4 copy-done.5
  154.5 14.3 %all_to_all.42.in_ref = bf16[16,72,256]{2,1,0:T(8,128)(2,1)} all-to-all(bf16[16,72,256]{2,1,0:T(8,128)(2,1)S(1)} %bitcast.24), channel_id=1, replica_groups=mesh['seq'=16,'head'=8] {'seq'}, dimensions={0} | all-to-all | bytes 1179648 | tf_op jit(solution)/shard_map/ffn_sum/all_to_all | solution.py:437
  168.7 2.0 ffn_sum.2
  170.7 13.6 %all_to_all.43 = bf16[16,72,256]{2,1,0:T(8,128)(2,1)} all-to-all(bf16[16,72,256]{2,1,0:T(8,128)(2,1)} %ffn_sum.2), channel_id=1, replica_groups=mesh['seq'=16,'head'=8] {'seq'}, dimensions={0} | all-to-all | bytes 1179648 | tf_op jit(solution)/shard_map/ffn_sum/all_to_all | solution.py:437
  184.3 0.0 all-gather.2.cloned.1.call-update
  184.3 5.7 %value_grad.2 = (bf16[1024,512]{1,0:T(8,128)(2,1)}, bf16[128,16,128]{2,1,0:T(8,128)(2,1)}) custom-call(s32[128]{0:T(128)} %lens_ref.9, bf16[16,64,512]{2,1,0:T(8,128)(2,1)} %tok_ref.7, bf16[16,64,512]{2,1,0:T(8,128)(2,1)} %copy-done, bf16[512]{0:T(512)(128)(2,1)} %gain_ref.10), custom_call_target="tpu_custom_call" | custom-call | flops 536870912 | bytes 4000000 | tf_op jit(solution)/shard_map/value_grad/pallas_call | solution.py:633
  190.0 8.4 %all-to-all-start.4 = ((bf16[128,16,128]{2,1,0:T(8,128)(2,1)}), bf16[128,16,128]{2,1,0:T(8,128)(2,1)S(1)}, u32[]{:S(2)}, u32[]{:S(2)}) async-start(bf16[128,16,128]{2,1,0:T(8,128)(2,1)} %get-tuple-element.48), calls=%async_computation.5 | async-start | bytes 1048576 | tf_op jit(solution)/shard_map/value_grad/all_to_all | solution.py:441
  198.4 13.8 %all-to-all-done.4.in_ref = bf16[128,16,128]{2,1,0:T(8,128)(2,1)S(1)} async-done(((bf16[128,16,128]{2,1,0:T(8,128)(2,1)}), bf16[128,16,128]{2,1,0:T(8,128)(2,1)S(1)}, u32[]{:S(2)}, u32[]{:S(2)}) %all-to-all-start.4) | async-done | bytes 524320 | tf_op jit(solution)/shard_map/value_grad/all_to_all | solution.py:441
  212.2 0.8 copy-done.2
  213.0 2.0 value_grad.3
  215.0 4.6 %all-to-all-start.5 = ((bf16[128,16,128]{2,1,0:T(8,128)(2,1)}), bf16[128,16,128]{2,1,0:T(8,128)(2,1)S(1)}, u32[]{:S(2)}, u32[]{:S(2)}) async-start(bf16[128,16,128]{2,1,0:T(8,128)(2,1)} %value_grad.3), calls=%async_computation.6 | async-start | bytes 1048576 | tf_op jit(solution)/shard_map/value_grad/all_to_all | solution.py:441
  219.7 0.0 reduce-scatter.5.cloned.1.call-done
  219.7 0.9 dynamic-slice_bitcast_fusion
  220.6 1.5 collective-permute-start.9
  222.1 7.1 %collective-permute-done.9 = bf16[64,1024]{1,0:T(8,128)(2,1)S(1)} collective-permute-done((bf16[64,1024]{1,0:T(8,128)(2,1)S(1)}, bf16[64,1024]{1,0:T(8,128)(2,1)S(1)}, u32[]{:S(2)}, u32[]{:S(2)}) %collective-permute-start.9) | collective-permute-done | bytes 131104 | tf_op jit(solution)/shard_map/logits_grad/ppermute | solution.py:426
  229.2 0.9 fusion
  230.2 5.9 %collective-permute-start.10 = (bf16[64,1024]{1,0:T(8,128)(2,1)S(1)}, bf16[64,1024]{1,0:T(8,128)(2,1)S(1)}, u32[]{:S(2)}, u32[]{:S(2)}) collective-permute-start(bf16[64,1024]{1,0:T(8,128)(2,1)S(1)} %fusion), channel_id=1, source_target_pairs={{0,0},{16,1},{32,2},{48,3},{64,4},{80,5},{96,6},{112,7},{8,8},{24,... | collective-permute-start | bytes 393224 | tf_op jit(solution)/shard_map/logits_grad/ppermute | solution.py:433
  236.1 0.1 reduce_max.14
  236.2 5.2 %input_grad.1 = f32[16,64,512]{2,1,0:T(8,128)} custom-call(bf16[16,64,512]{2,1,0:T(8,128)(2,1)} %tok_ref.7, bf16[1024,512]{1,0:T(8,128)(2,1)} %get-tuple-element.46.vgrad_ref, f32[1024,512]{1,0:T(8,128)} %get-tuple-element.47.gr_ref, bf16[512]{0:T(512)(128)(2,1)} %gain_ref.10, bf16[512,512]{1,0:T(8,128)(2,1)} %vw_ref.5), custom_call_target="tpu_custom_call" | custom-call | flops 536870912 | bytes 7000000 | tf_op jit(solution)/shard_map/input_grad/pallas_call | solution.py:656
  241.4 0.0 all-to-all-done.5.in_ref
  241.4 0.8 copy-done.1
  242.2 2.3 value_sum.1
  244.5 0.0 collective-permute-done.10
  244.5 0.8 multiply_bitcast_fusion
  245.4 7.7 %ffn_sum.3 = (f32[2048,512]{1,0:T(8,128)}, f32[512,2048]{1,0:T(8,128)}, f32[512,512]{1,0:T(8,128)}, f32[1,512]{1,0:T(1,128)}) custom-call(bf16[9216,256]{1,0:T(8,128)(2,1)} %all-gather.2.cloned.1.call-done.down_one.down_two.up_in.ow_one.ow_two, bf16[9216,256]{1,0:T(8,128)(2,1)} %all-gather.2.cloned.1.call-done.down_one.down_two.up_in.ow_one.ow_two, ...), custom_call_target="tpu_custom_call" | custom-call | flops 4000000 | bytes 13000000 | tf_op jit(solution)/shard_map/ffn_sum/pallas_call | solution.py:675
  (27 shorter events, 0.1 us)
Async XLA Ops:
  7.2 11.5 %collective-permute-start.1 = (bf16[64,1024]{1,0:T(8,128)(2,1)}, bf16[64,1024]{1,0:T(8,128)(2,1)S(1)}, u32[]{:S(2)}, u32[]{:S(2)}) collective-permute-start(bf16[64,1024]{1,0:T(8,128)(2,1)} %bitcast.25), channel_id=1, source_target_pairs={{0,8},{1,24},{2,40},{3,56},{4,72},{5,88},{6,104},{7,120},{8,0},{9,... | collective-permute-start | bytes 393224 | tf_op jit(solution)/shard_map/logits/ppermute | solution.py:433
  11.4 8.8 %collective-permute-start = (bf16[64,1024]{1,0:T(8,128)(2,1)}, bf16[64,1024]{1,0:T(8,128)(2,1)S(1)}, u32[]{:S(2)}, u32[]{:S(2)}) collective-permute-start(bf16[64,1024]{1,0:T(8,128)(2,1)} %bitcast.26), channel_id=1, source_target_pairs={{0,0},{1,16},{2,32},{3,48},{4,64},{5,80},{6,96},{7,112},{8,8},{9,2... | collective-permute-start | bytes 393224 | tf_op jit(solution)/shard_map/logits/ppermute | solution.py:433
  20.2 32.2 %all-to-all-start = ((bf16[16,64,512]{2,1,0:T(8,128)(2,1)}), bf16[16,64,512]{2,1,0:T(8,128)(2,1)S(1)}, u32[]{:S(2)}, u32[]{:S(2)}) async-start(bf16[16,64,512]{2,1,0:T(8,128)(2,1)} %values.1), calls=%async_computation | async-start | bytes 2097152 | tf_op jit(solution)/shard_map/values/all_to_all | solution.py:437
  32.8 120.2 %reduce-scatter.3.cloned.1.call-start = ((), (), s32[]{:S(2)}) async-start(), calls=%async_computation.10 | async-start | bytes 5308416 | tf_op jit(solution)/shard_map/ffn_sum/reduce_scatter | solution.py:587
  32.9 19.5 %copy-start.7 = (bf16[128,1024]{1,0:T(8,128)(2,1)}, bf16[128,1024]{1,0:T(8,128)(2,1)S(1)}, u32[]{:S(2)}) copy-start(bf16[128,1024]{1,0:T(8,128)(2,1)S(1)} %constant_dynamic-update-slice_fusion.refs_0_) | copy-start | bytes 786436
  32.9 10.2 %collective-permute-start.4 = (bf16[128,1024]{1,0:T(8,128)(2,1)S(1)}, bf16[128,1024]{1,0:T(8,128)(2,1)S(1)}, u32[]{:S(2)}, u32[]{:S(2)}) collective-permute-start(bf16[128,1024]{1,0:T(8,128)(2,1)S(1)} %constant_dynamic-update-slice_fusion.refs_0_), channel_id=1, source_target_pairs={{0,6},{1,7},{2,0},{3,1},{4,2},{5,3},{6,4},{7,5},{8,14},{9,15},{10,... | collective-permute-start | bytes 786440 | tf_op jit(solution)/shard_map/logits/ppermute | solution.py:421
  35.7 12.1 %collective-permute-start.3 = (bf16[128,1024]{1,0:T(8,128)(2,1)S(1)}, bf16[128,1024]{1,0:T(8,128)(2,1)S(1)}, u32[]{:S(2)}, u32[]{:S(2)}) collective-permute-start(bf16[128,1024]{1,0:T(8,128)(2,1)S(1)} %constant_dynamic-update-slice_fusion.refs_0_), channel_id=1, source_target_pairs={{0,4},{1,5},{2,6},{3,7},{4,0},{5,1},{6,2},{7,3},{8,12},{9,13},{10,... | collective-permute-start | bytes 786440 | tf_op jit(solution)/shard_map/logits/ppermute | solution.py:421
  35.7 14.7 %collective-permute-start.2 = (bf16[128,1024]{1,0:T(8,128)(2,1)S(1)}, bf16[128,1024]{1,0:T(8,128)(2,1)S(1)}, u32[]{:S(2)}, u32[]{:S(2)}) collective-permute-start(bf16[128,1024]{1,0:T(8,128)(2,1)S(1)} %constant_dynamic-update-slice_fusion.refs_0_), channel_id=1, source_target_pairs={{0,2},{1,3},{2,4},{3,5},{4,6},{5,7},{6,0},{7,1},{8,10},{9,11},{10,... | collective-permute-start | bytes 786440 | tf_op jit(solution)/shard_map/logits/ppermute | solution.py:421
  36.4 14.9 %collective-permute-start.5 = (bf16[128,1024]{1,0:T(8,128)(2,1)S(1)}, bf16[128,1024]{1,0:T(8,128)(2,1)S(1)}, u32[]{:S(2)}, u32[]{:S(2)}) collective-permute-start(bf16[128,1024]{1,0:T(8,128)(2,1)S(1)} %constant_dynamic-update-slice_fusion.refs_0_), channel_id=1, source_target_pairs={{0,1},{1,0},{2,3},{3,2},{4,5},{5,4},{6,7},{7,6},{8,9},{9,8},{10,11... | collective-permute-start | bytes 786440 | tf_op jit(solution)/shard_map/logits/ppermute | solution.py:426
  43.1 9.3 %copy-start.8 = (bf16[128,1024]{1,0:T(8,128)(2,1)}, bf16[128,1024]{1,0:T(8,128)(2,1)S(1)}, u32[]{:S(2)}) copy-start(bf16[128,1024]{1,0:T(8,128)(2,1)S(1)} %collective-permute-done.4.refs_3_) | copy-start | bytes 786436
  43.1 8.2 %collective-permute-start.8 = (bf16[128,1024]{1,0:T(8,128)(2,1)S(1)}, bf16[128,1024]{1,0:T(8,128)(2,1)S(1)}, u32[]{:S(2)}, u32[]{:S(2)}) collective-permute-start(bf16[128,1024]{1,0:T(8,128)(2,1)S(1)} %collective-permute-done.4.refs_3_), channel_id=1, source_target_pairs={{0,1},{1,0},{2,3},{3,2},{4,5},{5,4},{6,7},{7,6},{8,9},{9,8},{10,11... | collective-permute-start | bytes 786440 | tf_op jit(solution)/shard_map/logits/ppermute | solution.py:426
  47.9 4.6 %copy-start.9 = (bf16[128,1024]{1,0:T(8,128)(2,1)}, bf16[128,1024]{1,0:T(8,128)(2,1)S(1)}, u32[]{:S(2)}) copy-start(bf16[128,1024]{1,0:T(8,128)(2,1)S(1)} %collective-permute-done.3.refs_2_) | copy-start | bytes 786436
  47.9 3.4 %collective-permute-start.7 = (bf16[128,1024]{1,0:T(8,128)(2,1)S(1)}, bf16[128,1024]{1,0:T(8,128)(2,1)S(1)}, u32[]{:S(2)}, u32[]{:S(2)}) collective-permute-start(bf16[128,1024]{1,0:T(8,128)(2,1)S(1)} %collective-permute-done.3.refs_2_), channel_id=1, source_target_pairs={{0,1},{1,0},{2,3},{3,2},{4,5},{5,4},{6,7},{7,6},{8,9},{9,8},{10,11... | collective-permute-start | bytes 786440 | tf_op jit(solution)/shard_map/logits/ppermute | solution.py:426
  50.4 2.0 copy-start.10
  50.4 2.0 collective-permute-start.6
  51.3 1.2 copy-start.11
  51.3 1.2 copy-start.12
  51.3 1.2 copy-start.13
  52.4 0.7 copy-start.14
  52.4 1.1 copy-start.3
  109.0 1.2 copy-start.4
  135.1 17.9 %all-to-all-start.3 = ((bf16[16,64,512]{2,1,0:T(8,128)(2,1)}), bf16[16,64,512]{2,1,0:T(8,128)(2,1)S(1)}, u32[]{:S(2)}, u32[]{:S(2)}) async-start(bf16[16,64,512]{2,1,0:T(8,128)(2,1)} %bitcast.23), calls=%async_computation.4 | async-start | bytes 2097152 | tf_op jit(solution)/shard_map/unmix/all_to_all | solution.py:437
  138.8 80.9 %reduce-scatter.5.cloned.1.call-start = ((), (), s32[]{:S(2)}) async-start(), calls=%async_computation.11 | async-start | bytes 2359296 | tf_op jit(solution)/shard_map/scores/reduce_scatter | solution.py:615
  153.0 17.7 %copy-start = (bf16[16,64,512]{2,1,0:T(8,128)(2,1)}, bf16[16,64,512]{2,1,0:T(8,128)(2,1)S(1)}, u32[]{:S(2)}) copy-start(bf16[16,64,512]{2,1,0:T(8,128)(2,1)S(1)} %all-to-all-done.3.vg_ref) | copy-start | bytes 3145732
  153.0 1.4 copy-start.5
  153.0 92.3 %all-gather.2.cloned.1.call-start = ((), (), s32[]{:S(2)}) async-start(), calls=%async_computation.12 | async-start | bytes 5308416 | tf_op jit(solution)/shard_map/ffn_sum/all_gather | solution.py:630
  190.0 46.1 %copy-start.6 = (bf16[1,64,1024]{2,1,0:T(8,128)(2,1)S(1)}, bf16[1,64,1024]{2,1,0:T(8,128)(2,1)}, u32[]{:S(2)}) copy-start(bf16[1,64,1024]{2,1,0:T(8,128)(2,1)} %param.14) | copy-start | bytes 393220
  190.0 22.2 %all-to-all-start.4 = ((bf16[128,16,128]{2,1,0:T(8,128)(2,1)}), bf16[128,16,128]{2,1,0:T(8,128)(2,1)S(1)}, u32[]{:S(2)}, u32[]{:S(2)}) async-start(bf16[128,16,128]{2,1,0:T(8,128)(2,1)} %get-tuple-element.48), calls=%async_computation.5 | async-start | bytes 1048576 | tf_op jit(solution)/shard_map/value_grad/all_to_all | solution.py:441
  212.2 0.8 copy-start.2
  215.0 26.4 %all-to-all-start.5 = ((bf16[128,16,128]{2,1,0:T(8,128)(2,1)}), bf16[128,16,128]{2,1,0:T(8,128)(2,1)S(1)}, u32[]{:S(2)}, u32[]{:S(2)}) async-start(bf16[128,16,128]{2,1,0:T(8,128)(2,1)} %value_grad.3), calls=%async_computation.6 | async-start | bytes 1048576 | tf_op jit(solution)/shard_map/value_grad/all_to_all | solution.py:441
  220.6 8.6 %collective-permute-start.9 = (bf16[64,1024]{1,0:T(8,128)(2,1)S(1)}, bf16[64,1024]{1,0:T(8,128)(2,1)S(1)}, u32[]{:S(2)}, u32[]{:S(2)}) collective-permute-start(bf16[64,1024]{1,0:T(8,128)(2,1)S(1)} %dynamic-slice_bitcast_fusion), channel_id=1, source_target_pairs={{0,8},{1,9},{2,10},{3,11},{4,12},{5,13},{6,14},{7,15},{8,0},{9,1},... | collective-permute-start | bytes 393224 | tf_op jit(solution)/shard_map/logits_grad/ppermute | solution.py:426
  230.2 14.4 %collective-permute-start.10 = (bf16[64,1024]{1,0:T(8,128)(2,1)S(1)}, bf16[64,1024]{1,0:T(8,128)(2,1)S(1)}, u32[]{:S(2)}, u32[]{:S(2)}) collective-permute-start(bf16[64,1024]{1,0:T(8,128)(2,1)S(1)} %fusion), channel_id=1, source_target_pairs={{0,0},{16,1},{32,2},{48,3},{64,4},{80,5},{96,6},{112,7},{8,8},{24,... | collective-permute-start | bytes 393224 | tf_op jit(solution)/shard_map/logits_grad/ppermute | solution.py:433
  241.4 0.8 copy-start.1
Sparse Core Ops, SparseCore 0:
  109.1 33.9 reduce-scatter.2
  153.2 30.1 reduce-scatter.4
  185.1 45.4 all-gather.1

commit v2 on v1

v2 whole, which is shorter than its diff:
```python
import functools
import math

import jax
import jax.numpy as jnp
from jax import lax
from jax.experimental import pallas as pl
from jax.experimental.pallas import tpu as pltpu
from jax.sharding import PartitionSpec as P

EPS = 1e-06
ROOT_HALF = 1.0 / math.sqrt(2.0)
DENSITY = 1.0 / math.sqrt(2.0 * math.pi)
LANES = 128
CHUNK = 32
PER = LANES // CHUNK
PLANE = ("x", "y")
CHIPS = ("x", "y", "z")
ALL = ("x", "y", "z", "core")
bf16 = jnp.bfloat16
f32 = jnp.float32


def nt(left, right):
    return lax.dot_general(left, right, (((1,), (1,)), ((), ())), preferred_element_type=f32)


def tn(left, right):
    return lax.dot_general(left, right, (((0,), (0,)), ((), ())), preferred_element_type=f32)


def nn(left, right):
    return jnp.dot(left, right, preferred_element_type=f32)


def lane_groups(rows):
    return lax.broadcasted_iota(jnp.int32, (rows, LANES), 1) // CHUNK


def pick(groups, parts):
    out = parts[PER - 1]
    for l in range(PER - 2, -1, -1):
        out = jnp.where(groups == l, parts[l], out)
    return out


def seat(chunk):
    return chunk % 4 * 4 + chunk // 4


def spread(value, store):
    rows = value.shape[0] // PER
    groups = lane_groups(rows)
    for q in range(value.shape[1] // LANES):
        turned = []
        for r in range(PER):
            piece = value[r * rows : (r + 1) * rows, q * LANES : (q + 1) * LANES]
            turned.append(pltpu.roll(piece, CHUNK * r, 1) if r else piece)
        for k in range(PER):
            store(seat(q * PER + k), pick(groups, [turned[(l - k) % PER] for l in range(PER)]))


def collect(ref, group):
    chunks, rows, _ = ref.shape
    lanes = slice(group * LANES, (group + 1) * LANES)
    groups = lane_groups(rows)
    columns = []
    for q in range(chunks // PER):
        loaded = [ref[seat(q * PER + k), :, lanes].astype(f32) for k in range(PER)]
        parts = []
        for r in range(PER):
            mixed = pick(groups, [loaded[(l - r) % PER] for l in range(PER)])
            parts.append(pltpu.roll(mixed, LANES - CHUNK * r, 1) if r else mixed)
        columns.append(jnp.concatenate(parts, axis=0))
    return jnp.concatenate(columns, axis=1)


def places():
    return tuple(lax.axis_index(axis) for axis in ALL)


def first_bucket(lens_ref):
    _, _, z, c = places()
    return (z * 2 + c) * (lens_ref.shape[0] // 8)


def row_keep(lens_ref, buckets, rows):
    x, y, _, _ = places()
    spot = (x * 4 + y) * rows + lax.broadcasted_iota(jnp.int32, (rows, 1), 0)
    first = first_bucket(lens_ref) + pl.program_id(0) * buckets
    parts = [(spot < lens_ref[first + r]).astype(f32) for r in range(buckets)]
    return jnp.concatenate(parts, axis=0)


def gain_row(gain_ref):
    return gain_ref[...].astype(f32).reshape(1, gain_ref.shape[0])


def rms(values):
    scale = lax.rsqrt(jnp.mean(values * values, axis=-1, keepdims=True) + EPS)
    return values * scale, scale


def values_kernel(lens_ref, tok_ref, gain_ref, vw_ref, out_ref):
    per, rows, width = tok_ref.shape
    tok = tok_ref[...].reshape(per * rows, width).astype(f32)
    normed, _ = rms(tok)
    hidden = (normed * gain_row(gain_ref)).astype(bf16)
    val = nn(hidden, vw_ref[...]) * row_keep(lens_ref, per, rows)

    def store(chunk, block):
        out_ref[chunk] = block.astype(bf16)

    spread(val, store)


def lane_lengths(lens_ref, lanes):
    x, _, _, _ = places()
    group = lanes // CHUNK
    first = first_bucket(lens_ref)
    lane = lax.broadcasted_iota(jnp.int32, (1, lanes), 1) // CHUNK
    lens = jnp.zeros((1, lanes), jnp.int32)
    for n in range(group):
        m, l = divmod(n, PER)
        lens = jnp.where(lane == n, lens_ref[first + m * PER + (l - x + PER) % PER], lens)
    return lens


def mix_kernel(lens_ref, *refs):
    count = len(refs) - 12
    pieces = refs[:count]
    held_ref, exp_out, inv_out, mix_out = refs[count : count + 4]
    landed, held, keep, expo, inverse, mixed, sems, out_sems = refs[count + 4 :]
    span, lanes = held.shape
    x, _, z, c = places()
    half = pieces[0].shape[0] // 2
    copies = [
        pltpu.make_async_copy(piece, landed.at[n], sems.at[n]) for n, piece in enumerate(pieces)
    ]
    held_copy = pltpu.make_async_copy(held_ref, held, sems.at[count])
    copies[0].start()
    held_copy.start()
    for copy in copies[1:]:
        copy.start()
    lens = lane_lengths(lens_ref, lanes)
    place = lax.broadcasted_iota(jnp.int32, (span, lanes), 0)
    keep[...] = (place < lens).astype(f32).astype(bf16)
    out_copies = []
    deep = 4 * 2 * half
    for batch in range(2):
        starts = []
        bounds = []
        for n in range(4 * batch, 4 * batch + 4):
            copies[n].wait()
            core = c if batch == 0 else 1 - c
            ring = (z - n % 4 + 4) % 4
            for k in range(2):
                start = ((core * 2 + (x + k) % 2) * 4 + ring) * half
                starts.append(pl.multiple_of(start, half))
                bounds.append(lens - start)
        cut = pl.ds(4 * batch, 4)
        logits = landed[cut].reshape(deep, span).astype(f32)
        part = jnp.exp(logits - jnp.max(logits, axis=-1, keepdims=True)).astype(bf16)
        expo[cut] = part.reshape(4, 2 * half, span)
        totals = nn(part, keep[...])
        row = lax.broadcasted_iota(jnp.int32, (half, lanes), 0)
        kept = jnp.concatenate([(row < bound).astype(f32) for bound in bounds], axis=0)
        inverted = kept / totals
        inverse[cut] = inverted.reshape(4, 2 * half, lanes)
        if batch == 0:
            held_copy.wait()
        mixed[cut] = (nn(part, held[...]) * inverted).astype(bf16).reshape(4, 2 * half, lanes)
        for n in range(4 * batch, 4 * batch + 4):
            for j, (source, target) in enumerate(
                ((mixed, mix_out), (expo, exp_out), (inverse, inv_out))
            ):
                for k in range(2):
                    copy = pltpu.make_async_copy(
                        source.at[n, pl.ds(k * half, half), :],
                        target.at[pl.ds(starts[2 * (n - 4 * batch) + k], half), :],
                        out_sems.at[n, j, k],
                    )
                    copy.start()
                    out_copies.append(copy)
    for copy in out_copies:
        copy.wait()


def unmix_kernel(exp_ref, gm_ref, inv_ref, mixed_ref, out_ref, g_ref, r_ref):
    @pl.when(pl.program_id(0) == 0)
    def _():
        scaled = gm_ref[...].astype(f32) * inv_ref[...]
        g_ref[...] = scaled.astype(bf16)
        r_ref[...] = (scaled * mixed_ref[...].astype(f32)).astype(bf16)

    out_ref[...] = tn(exp_ref[...], g_ref[...]).astype(bf16)


def scores_kernel(lens_ref, g_ref, r_ref, val_ref, own_ref, other_ref, keep_ref):
    span, lanes = val_ref.shape

    @pl.when(pl.program_id(0) == 0)
    def _():
        place = lax.broadcasted_iota(jnp.int32, (span, lanes), 0)
        keep_ref[...] = (place < lane_lengths(lens_ref, lanes)).astype(f32).astype(bf16)

    out = (nt(g_ref[...], val_ref[...]) - nt(r_ref[...], keep_ref[...])).astype(bf16)
    step = pl.program_id(0)
    _, _, _, c = places()
    rings, _, rows, _ = own_ref.shape

    def store(ref):
        for n in range(rings):
            ref[n, step % 2] = out[n * rows : (n + 1) * rows]

    @pl.when(step // 2 == c)
    def _():
        store(own_ref)

    @pl.when(step // 2 != c)
    def _():
        store(other_ref)


def ffn_kernel(
    lens_ref,
    tok_ref,
    cot_ref,
    mix_ref,
    ow_ref,
    gain_ref,
    up_ref,
    down_ref,
    out_ref,
    gr_ref,
    gm_ref,
    own_out,
    other_out,
    down_acc,
    up_acc,
    ow_acc,
):
    per, rows, width = tok_ref.shape
    n = per * rows
    ff = up_ref.shape[1]
    step = up_acc.shape[2]

    @pl.when(pl.program_id(0) == 0)
    def _():
        down_acc[...] = jnp.zeros_like(down_acc)
        up_acc[...] = jnp.zeros_like(up_acc)
        ow_acc[...] = jnp.zeros_like(ow_acc)

    keep = row_keep(lens_ref, per, rows)
    tok = tok_ref[...].reshape(n, width).astype(f32)
    grad_low = (cot_ref[...].reshape(n, width).astype(f32) * keep).astype(bf16)
    mixed = jnp.concatenate(
        [collect(mix_ref, g) for g in range(per // PER)], axis=0
    ).astype(bf16)
    resid = tok + nn(mixed, ow_ref[...])
    normed, scale = rms(resid)
    gain = gain_row(gain_ref)
    hidden = (normed * gain).astype(bf16)
    ffn = jnp.zeros((n, width), f32)
    grad_hidden = jnp.zeros((n, width), f32)
    for q in range(ff // step):
        cut = slice(q * step, (q + 1) * step)
        up = up_ref[:, cut]
        down = down_ref[cut, :]
        pre = nn(hidden, up)
        cdf = 0.5 * (1.0 + lax.erf(pre * ROOT_HALF))
        slope = cdf + pre * jnp.exp(-0.5 * pre * pre) * DENSITY
        act = (pre * cdf).astype(bf16)
        ffn = ffn + nn(act, down)
        grad_pre = (nt(grad_low, down) * slope).astype(bf16)
        grad_hidden = grad_hidden + nt(grad_pre, up)
        down_acc[cut, :] += tn(act, grad_low)
        up_acc[q] += tn(hidden, grad_pre)
    out_ref[...] = ((resid + ffn) * keep).astype(bf16).reshape(per, rows, width)
    weighted = grad_hidden * gain
    back = scale * (weighted - normed * jnp.mean(weighted * normed, axis=-1, keepdims=True))
    grad_resid = grad_low.astype(f32) + back
    gr_ref[...] = grad_resid
    grad_att = grad_resid.astype(bf16)
    ow_acc[...] += tn(mixed, grad_att)
    grad_mixed = nt(grad_att, ow_ref[...]) * keep
    size = PER * rows
    for g in range(per // PER):

        def store(chunk, block, g=g):
            gm_ref[chunk, :, g * LANES : (g + 1) * LANES] = block.astype(bf16)

        spread(grad_mixed[g * size : (g + 1) * size], store)

    @pl.when(pl.program_id(0) == pl.num_programs(0) - 1)
    def _():
        _, _, _, core = places()
        half = width // 2
        count, tall, _ = own_out.shape
        deep = tall - 2 * width
        for ref, side in ((other_out, 1 - core), (own_out, core)):
            lanes = pl.ds(pl.multiple_of(side * half, half), half)
            for n in range(count):
                ref[n, :width, :] = down_acc[n * width : (n + 1) * width, lanes].astype(bf16)
                ref[n, width : 2 * width, :] = up_acc[n, :, lanes].astype(bf16)
                ref[n, 2 * width :, :] = ow_acc[n * deep : (n + 1) * deep, lanes].astype(bf16)


def value_grad_kernel(lens_ref, tok_ref, vg_ref, gain_ref, ffn_ref, vgrad_ref, joint_ref, acc_ref):
    per, rows, width = tok_ref.shape
    tok = tok_ref[...].reshape(per * rows, width).astype(f32)
    normed, _ = rms(tok)
    hidden = (normed * gain_row(gain_ref)).astype(bf16)
    vgrad = (collect(vg_ref, 0) * row_keep(lens_ref, per, rows)).astype(bf16)
    vgrad_ref[...] = vgrad

    @pl.when(pl.program_id(0) == 0)
    def _():
        acc_ref[...] = jnp.zeros_like(acc_ref)

    acc_ref[...] += tn(hidden, vgrad)

    @pl.when(pl.program_id(0) == pl.num_programs(0) - 1)
    def _():
        count, tall, half = joint_ref.shape
        deep = ffn_ref.shape[1]
        rows_here = (tall - deep) // 2
        joint_ref[:, :deep, :] = ffn_ref[...]
        for n in range(count):
            for k in range(2):
                joint_ref[n, deep + k * rows_here : deep + (k + 1) * rows_here, :] = acc_ref[
                    n * rows_here : (n + 1) * rows_here, k * half : (k + 1) * half
                ].astype(bf16)


def input_grad_kernel(tok_ref, vgrad_ref, gr_ref, gain_ref, vw_ref, out_ref):
    per, rows, width = tok_ref.shape
    tok = tok_ref[...].reshape(per * rows, width).astype(f32)
    normed, scale = rms(tok)
    weighted = nt(vgrad_ref[...], vw_ref[...]) * gain_row(gain_ref)
    back = scale * (weighted - normed * jnp.mean(weighted * normed, axis=-1, keepdims=True))
    out_ref[...] = (gr_ref[...] + back).reshape(per, rows, width)


def joint_sum_kernel(joint_ref, ffn_ref, value_ref):
    total = jnp.sum(joint_ref[...].astype(f32), axis=0).astype(bf16)
    deep = ffn_ref.shape[1]
    ffn_ref[...] = jnp.broadcast_to(total[None, :deep], ffn_ref.shape)
    value_ref[...] = total[deep:]


def ring_spread_kernel(*refs):
    parts, out_ref, held = refs[:4], refs[4], refs[5]
    me = lax.axis_index("z")
    for k, part in enumerate(parts):
        held[(me - k + 4) % 4] = part[...].astype(f32)
    total = (held[0] + held[1]) + (held[2] + held[3])
    out_ref[...] = jnp.broadcast_to(total[None], out_ref.shape).astype(bf16)


def row_total(product):
    folded = sum(
        product[:, n * LANES : (n + 1) * LANES] for n in range(product.shape[1] // LANES)
    )
    return jnp.sum(folded.T, axis=0, keepdims=True)


def fold_kernel(own_ref, got_ref, *outs):
    step = pl.program_id(0)
    total = (own_ref[0].astype(f32) + got_ref[0].astype(f32)).astype(bf16)
    for k, out in enumerate(outs):

        @pl.when(step == k)
        def _(out=out):
            out[...] = total


def sum_kernel(*refs):
    parts, out_ref = refs[:-1], refs[-1]
    out_ref[...] = sum(part[...].astype(f32) for part in parts).astype(bf16)


def split_sum_kernel(*refs):
    parts, (own_ref, other_ref) = refs[:4], refs[4:]
    total = sum(part[...].astype(f32) for part in parts).astype(bf16)
    odd = places()[0] % 2 == 1
    own_ref[...] = jnp.where(odd, total[1], total[0])
    other_ref[...] = jnp.where(odd, total[0], total[1])


def logits_grad_kernel(part_ref, logits_ref, out_ref):
    logits = logits_ref[0].astype(f32)
    exact = jnp.exp(logits - jnp.max(logits, axis=-1, keepdims=True))
    out_ref[0] = part_ref[...].astype(f32) * exact


def finish_ffn_kernel(*refs):
    pieces, (up_ref, gain_ref), (down_out, up_out, ow_out, gain_out) = refs[:8], refs[8:10], refs[10:14]
    landed, wide, up, sems, out_sems = refs[14:]
    width = up.shape[0]
    half = landed.shape[2]
    deep = landed.shape[1] - 2 * width
    _, _, z, c = places()
    copies = [
        pltpu.make_async_copy(piece, landed.at[n], sems.at[n]) for n, piece in enumerate(pieces)
    ]
    up_copy = pltpu.make_async_copy(up_ref, up, sems.at[8])
    copies[0].start()
    up_copy.start()
    for copy in copies[1:]:
        copy.start()
    product = jnp.zeros((width, half), f32)
    out_copies = []
    for n, copy in enumerate(copies):
        copy.wait()
        ring = (z - n % 4 + 4) % 4
        side = c if n < 4 else 1 - c
        wide[n] = landed[n].astype(f32)
        lanes = pl.ds(pl.multiple_of(side * half, half), half)
        columns = pl.ds(pl.multiple_of((2 * ring + side) * half, half), half)
        targets = (
            (0, width, down_out.at[pl.ds(pl.multiple_of(ring * width, width), width), lanes]),
            (width, width, up_out.at[:, columns]),
            (2 * width, deep, ow_out.at[pl.ds(pl.multiple_of(ring * deep, deep), deep), lanes]),
        )
        for k, (first, tall, target) in enumerate(targets):
            out_copy = pltpu.make_async_copy(
                wide.at[n, pl.ds(first, tall), :], target, out_sems.at[n, k]
            )
            out_copy.start()
            out_copies.append(out_copy)
        if n == 0:
            up_copy.wait()
        product = product + up[:, columns].astype(f32) * wide[n, width : 2 * width, :]
    gain_out[...] = row_total(product) / gain_row(gain_ref)
    for out_copy in out_copies:
        out_copy.wait()


def finish_value_kernel(in_ref, vw_ref, gain_ref, out_ref, gain_out):
    count, tall, half = in_ref.shape
    rows_here = tall // 2
    for n in range(count):
        for k in range(2):
            out_ref[n * rows_here : (n + 1) * rows_here, k * half : (k + 1) * half] = in_ref[
                n, k * rows_here : (k + 1) * rows_here
            ].astype(f32)
    gain_out[...] = row_total(vw_ref[...].astype(f32) * out_ref[...]) / gain_row(gain_ref)


def params():
    return pltpu.CompilerParams(vmem_limit_bytes=63 * 1024 * 1024)


def cost(flops, size):
    return pl.CostEstimate(flops=int(flops), bytes_accessed=int(size), transcendentals=0)


def whole(*shape):
    return pl.BlockSpec(shape, lambda *_: (0,) * len(shape))


def once(*shape):
    return pl.BlockSpec(shape, lambda *_: (0,) * len(shape), pipeline_mode=pl.Buffered(1))


def shaped(dtype, *shape):
    return pltpu.HBM(shape, dtype)


def stay(*arrays):
    return [pltpu.with_memory_space_constraint(array, pltpu.HBM) for array in arrays]


def flat(x, y, z, c):
    return ((x % 4) * 4 + y % 4) * 8 + (z % 4) * 2 + c % 2


def devices():
    for i in range(128):
        s, h = divmod(i, 8)
        yield i, s // 4, s % 4, h // 2, h % 2


def shift(array, axis, step):
    return lax.ppermute(array, axis, [(i, (i + step) % 4) for i in range(4)])


def flip(array):
    return lax.ppermute(array, "core", [(0, 1), (1, 0)])


def flip_x(array):
    return lax.ppermute(array, "x", [(i, i ^ 1) for i in range(4)])


def to_plane(array, back=False):
    pairs = [(i, flat(2 * e + (a & 1), d, b, a >> 1)) for i, a, b, d, e in devices()]
    if back:
        pairs = [(j, i) for i, j in pairs]
    return lax.ppermute(array, ALL, pairs)


def around(parts, axis):
    return [parts[0]] + [shift(parts[step], axis, step) for step in (1, 2, 3)]


def swap(array, axes):
    return lax.all_to_all(array, axes, 0, 0, tiled=True)


def swap_seq(array):
    return swap(array, PLANE)


def after(array, *others):
    return lax.optimization_barrier((array,) + others)[0]


def ordered(arrays, *others):
    return list(lax.optimization_barrier((*arrays, *others)))[: len(arrays)]


def shards(
    tokens,
    lengths,
    norm_gain,
    value_weight,
    synth_logits,
    out_weight,
    ffn_gain,
    up_weight,
    down_weight,
    cotangent,
):
    group, rows, width = tokens.shape
    span = synth_logits.shape[2]
    ff = up_weight.shape[1]
    blocks = span // rows
    total_rows = group * rows
    steps = group // PER
    tile = PER * rows

    def tok_spec(n):
        return pl.BlockSpec((n, rows, width), lambda m, *_: (m, 0, 0))

    def move_spec(n):
        return pl.BlockSpec((blocks, rows, n // PER * LANES), lambda m, *_: (0, 0, m))

    def row_spec(n, columns):
        return pl.BlockSpec((n, columns), lambda m, *_: (m, 0))

    def call(kernel, grid, ins, outs, shapes, flops, size, scratch=(), prefetch=0, long=False):
        return pl.pallas_call(
            kernel,
            grid_spec=pltpu.PrefetchScalarGridSpec(
                num_scalar_prefetch=prefetch,
                grid=grid,
                in_specs=ins,
                out_specs=outs,
                scratch_shapes=scratch,
            ),
            out_shape=shapes,
            compiler_params=params(),
            cost_estimate=cost(1e13, 1e6) if long else cost(1e6, 1e5),
        )

    with jax.named_scope("logits"):
        block = synth_logits.reshape(rows, span)
        block = to_plane(block)

    with jax.named_scope("values"):
        sent_values = call(
            values_kernel,
            (steps,),
            [tok_spec(PER), whole(width), whole(width, width)],
            move_spec(PER),
            shaped(bf16, blocks, rows, width),
            2 * total_rows * width * width,
            3e6,
            prefetch=1,
        )(lengths, *stay(tokens, norm_gain, value_weight))
        block = ordered([block], sent_values)[0]

    with jax.named_scope("logits"):
        other = flip_x(block)
        pair = jnp.concatenate([block, other])
        held = swap_seq(ordered([sent_values], other)[0]).reshape(span, width)
        pieces = [pair] + [shift(pair, "z", step) for step in (1, 2, 3)]
        pieces = pieces + [flip(piece) for piece in pieces]

    quarter = span // 4
    anywhere = pl.BlockSpec(memory_space=pl.ANY)
    with jax.named_scope("mix"):
        expo, inverse, mixed_held = call(
            mix_kernel,
            (1,),
            [anywhere] * 9,
            [anywhere] * 3,
            [shaped(bf16, span, span), shaped(f32, span, width), shaped(bf16, span, width)],
            4 * span * span * width,
            8e6,
            scratch=[
                pltpu.VMEM((8, 2 * rows, span), bf16),
                pltpu.VMEM((span, width), bf16),
                pltpu.VMEM((span, width), bf16),
                pltpu.VMEM((8, 2 * rows, span), bf16),
                pltpu.VMEM((8, 2 * rows, width), f32),
                pltpu.VMEM((8, 2 * rows, width), bf16),
                pltpu.SemaphoreType.DMA((9,)),
                pltpu.SemaphoreType.DMA((8, 3, 2)),
            ],
            prefetch=1,
        )(lengths, *pieces, held)
        got_mixed = swap_seq(mixed_held.reshape(blocks, rows, width))

    tall = ff // 4 + width + width // 4
    half_width = width // 2
    grads_shape = (4, tall, half_width)
    with jax.named_scope("ffn"):
        output, grad_resid, sent_grad, own_part, other_part = call(
            ffn_kernel,
            (steps // 2,),
            [
                tok_spec(2 * PER),
                tok_spec(2 * PER),
                move_spec(2 * PER),
                once(width, width),
                once(width),
                once(width, ff),
                once(ff, width),
            ],
            [
                tok_spec(2 * PER),
                row_spec(2 * tile, width),
                move_spec(2 * PER),
                once(*grads_shape),
                once(*grads_shape),
            ],
            [
                shaped(bf16, group, rows, width),
                shaped(f32, total_rows, width),
                shaped(bf16, blocks, rows, width),
                shaped(bf16, *grads_shape),
                shaped(bf16, *grads_shape),
            ],
            2 * total_rows * width * (6 * ff + 3 * width),
            2e7,
            scratch=[
                pltpu.VMEM((ff, width), f32),
                pltpu.VMEM((ff // width, width, width), f32),
                pltpu.VMEM((width, width), f32),
            ],
            prefetch=1,
        )(
            lengths,
            *stay(tokens, cotangent), got_mixed, *stay(out_weight, ffn_gain, up_weight, down_weight),
        )
        got_grad = swap_seq(sent_grad).reshape(span, width)

    def fold(own, got):
        shape = own.shape[1:]
        zeros = (0,) * len(shape)
        part = pl.BlockSpec((1,) + shape, lambda k: ((lax.axis_index("z") + k) % 4,) + zeros)
        return call(
            fold_kernel,
            (4,),
            [part] * 2,
            [whole(*shape)] * 4,
            [shaped(bf16, *shape)] * 4,
            1e6,
            6 * math.prod(own.shape),
        )(*stay(own), got)

    with jax.named_scope("ffn_sum"):
        folded = fold(own_part, flip(other_part))
        ring_parts = around(folded, "z")
        got_grad = ordered([got_grad], folded[0])[0]

    with jax.named_scope("unmix"):
        held_grad, g_scaled, r_scaled = call(
            unmix_kernel,
            (4,),
            [pl.BlockSpec((span, quarter), lambda j: (0, j))] + [once(span, width)] * 3,
            [row_spec(quarter, width), whole(span, width), whole(span, width)],
            [shaped(bf16, span, width)] * 3,
            2 * span * span * width,
            9e6,
        )(*stay(expo), got_grad, *stay(inverse, mixed_held))
        got_values = swap_seq(held_grad.reshape(blocks, rows, width))


    with jax.named_scope("scores"):
        score_shape = (4, 2, rows, span)
        own_scores, other_scores = call(
            scores_kernel,
            (4,),
            [row_spec(quarter, width), row_spec(quarter, width), whole(span, width)],
            [whole(*score_shape)] * 2,
            [shaped(bf16, *score_shape)] * 2,
            4 * span * span * width,
            8e6,
            scratch=[pltpu.VMEM((span, width), bf16)],
            prefetch=1,
        )(lengths, *stay(g_scaled, r_scaled), ordered([held], held_grad)[0])
        got_scores = flip(other_scores)

    with jax.named_scope("ffn_sum"):
        part = row_spec(tall // 4, half_width)
        ring_parts = ordered(ring_parts, own_scores)
        ffn_sum = call(
            sum_kernel,
            (4,),
            [part] * 4,
            part,
            shaped(bf16, tall, half_width),
            1e6,
            3e6,
            long=True,
        )(*ring_parts)

    with jax.named_scope("score_sum"):
        score_parts = fold(*ordered([own_scores, got_scores], ffn_sum))
        score_ring = around(score_parts, "z")
        got_values = ordered([got_values], score_parts[0])[0]

    with jax.named_scope("ffn_sum"):
        piece = tall // blocks
        ffn_sum = ffn_sum.reshape(blocks, piece, half_width)
        joint = piece + 2 * (width // blocks)

    with jax.named_scope("value_grad"):
        value_grad, joint_part = call(
            value_grad_kernel,
            (steps,),
            [tok_spec(PER), move_spec(PER), whole(width), whole(blocks, piece, half_width)],
            [row_spec(tile, width), whole(blocks, joint, half_width)],
            [shaped(bf16, total_rows, width), shaped(bf16, blocks, joint, half_width)],
            2 * total_rows * width * width,
            4e6,
            scratch=[pltpu.VMEM((width, width), f32)],
            prefetch=1,
        )(lengths, *stay(tokens), got_values, *stay(norm_gain), ffn_sum)
        got_joint = swap_seq(joint_part)

    with jax.named_scope("score_sum"):
        own_scores, other_scores = call(
            split_sum_kernel,
            (1,),
            [whole(2, rows, span)] * 4,
            [whole(rows, span)] * 2,
            [shaped(bf16, rows, span)] * 2,
            1e6,
            2e6,
            long=True,
        )(*ordered(score_ring, joint_part))
        got_scores = flip_x(other_scores)

    with jax.named_scope("input_grad"):
        input_grad = call(
            input_grad_kernel,
            (steps,),
            [
                tok_spec(PER),
                row_spec(tile, width),
                row_spec(tile, width),
                whole(width),
                whole(width, width),
            ],
            tok_spec(PER),
            shaped(f32, group, rows, width),
            2 * total_rows * width * width,
            7e6,
        )(*stay(tokens), value_grad, *stay(*ordered([grad_resid], own_scores), norm_gain, value_weight))

    with jax.named_scope("score_sum"):
        score_total = call(
            sum_kernel,
            (1,),
            [whole(rows, span)] * 2,
            whole(rows, span),
            shaped(bf16, rows, span),
            1e6,
            1e6,
        )(*ordered([own_scores, got_scores], input_grad))
        score_back = to_plane(score_total, back=True)

    with jax.named_scope("joint_sum"):
        few = (joint - piece, half_width)
        ffn_spread, small = call(
            joint_sum_kernel,
            (1,),
            [whole(blocks, joint, half_width)],
            [whole(blocks, piece, half_width), whole(*few)],
            [shaped(bf16, blocks, piece, half_width), shaped(bf16, *few)],
            1e6,
            2e6,
        )(*ordered([got_joint], score_total))

    with jax.named_scope("value_sum"):
        small = call(
            sum_kernel,
            (1,),
            [whole(*few)] * 2,
            whole(*few),
            shaped(bf16, *few),
            1e6,
            1e6,
        )(small, flip(small))
        value_spread = call(
            ring_spread_kernel,
            (1,),
            [whole(*few)] * 4,
            whole(blocks, *few),
            shaped(bf16, blocks, *few),
            1e6,
            1e6,
            scratch=[pltpu.VMEM((4, *few), f32)],
        )(*around([small] * 4, "z"))

    with jax.named_scope("score_sum"):
        logits_grad = call(
            logits_grad_kernel,
            (1,),
            [whole(rows, span), whole(1, rows, span)],
            whole(1, rows, span),
            shaped(f32, 1, rows, span),
            1e6,
            1e6,
        )(*ordered([score_back], value_spread), synth_logits)

    with jax.named_scope("ffn_sum"):
        ffn_sum = ordered([swap_seq(ffn_spread)], value_spread)[0].reshape(tall, half_width)
        pieces = around([ffn_sum] * 4, "z")

    with jax.named_scope("value_sum"):
        value_sum = swap_seq(ordered([value_spread], ffn_sum)[0])

    with jax.named_scope("value_sum"):
        value_weight_grad, norm_gain_grad = call(
            finish_value_kernel,
            (1,),
            [whole(blocks, *few), whole(width, width), whole(width)],
            [whole(width, width), whole(1, width)],
            [shaped(f32, width, width), shaped(f32, 1, width)],
            4e6,
            2e6,
        )(value_sum, *stay(value_weight, norm_gain))

    with jax.named_scope("ffn_sum"):
        pieces = ordered(pieces, value_weight_grad, logits_grad)
        pieces = pieces + [flip(part) for part in pieces]
        down_grad, up_grad, out_grad, ffn_gain_grad = call(
            finish_ffn_kernel,
            (1,),
            [anywhere] * 9 + [whole(width)],
            [anywhere] * 3 + [whole(1, width)],
            [
                shaped(f32, ff, width),
                shaped(f32, width, ff),
                shaped(f32, width, width),
                shaped(f32, 1, width),
            ],
            4e6,
            13e6,
            scratch=[
                pltpu.VMEM((8, tall, half_width), bf16),
                pltpu.VMEM((8, tall, half_width), f32),
                pltpu.VMEM((width, ff), bf16),
                pltpu.SemaphoreType.DMA((9,)),
                pltpu.SemaphoreType.DMA((8, 3)),
            ],
        )(*pieces, *stay(up_weight, ffn_gain))

    return (
        output,
        input_grad,
        norm_gain_grad.reshape(width),
        value_weight_grad,
        logits_grad,
        out_grad,
        ffn_gain_grad.reshape(width),
        up_grad,
        down_grad,
    )


def solution(mesh):
    token_spec = P(("z", "core"), PLANE, None)
    placed = (
        token_spec,
        P(),
        P(),
        P(),
        token_spec,
        P(),
        P(),
        P(),
        P(),
        token_spec,
    )
    fine = jax.sharding.Mesh(mesh.devices.reshape(4, 4, 4, 2), ALL)
    return jax.shard_map(
        shards,
        mesh=fine,
        in_specs=placed,
        out_specs=(token_spec, token_spec, P(), P(), token_spec, P(), P(), P(), P()),
        check_vma=False,
    )
```

time: 263 us -> 257 us (0.977)
  blocking collectives: 69 us -> 22.5 us
  starting transfers between devices: 54.2 us -> 90.2 us
  Pallas kernels: 75.9 us -> 95.3 us
  between operations: 14 us -> 1.09 us
  local copies, waits for them, and re-layouts: 6.12 us -> 8.78 us
    all_to_all x4 -> x1, blocking collectives: 69 us -> 22.5 us  [swap(): return lax.all_to_all(array, axes, 0, 0, tiled=True)]
    ppermute x11 -> x30, starting transfers between devices: 24.8 us -> 51.7 us  [the longest x11 21.5 us: flip(): return lax.ppermute(array, 'core', [(0, 1), (1, 0)])]
    pallas_call x5 -> x12, Pallas kernels: 20.4 us -> 38.9 us  [the longest x2 8.64 us: fold(): call(fold_kernel, (4,), [part] * 2, [whole(*shape)] * 4, [shaped(bf16, *s...]
    all_to_all x4 -> x6, waiting for transfers between devices: 21.3 us -> 9.15 us  [swap(): return lax.all_to_all(array, axes, 0, 0, tiled=True)]
    ppermute x11 -> x30, waiting for transfers between devices: 17 us -> 28.5 us  [the longest x15 11.4 us: shift(): return lax.ppermute(array, axis, [(i, (i + step) % 4) for i in range(4)])]
    all_to_all x4 -> x6, starting transfers between devices: 29.3 us -> 38.5 us  [swap(): return lax.all_to_all(array, axes, 0, 0, tiled=True)]
    unnamed x31 -> x45, local copies, waits for them, and re-layouts: 5.18 us -> 8.76 us
  transfers between devices with their start and end apart: 18 -> 36, of which waited for: 7 -> 13; matrix products, arithmetic and copies ran while one was open for 1% -> 0% of each run, Pallas kernels for 14% -> 21%
where the time goes in v2:
time: 257 us; the launch traced here: 256 us
  Pallas kernels  95.3 us (37%)
  starting transfers between devices  90.2 us (35%)
  waiting for transfers between devices  37.7 us (15%)
  blocking collectives  22.5 us (9%)
  local copies, waits for them, and re-layouts  8.78 us (3%)
    all_to_all x6, starting transfers between devices, swap(): return lax.all_to_all(array, axes, 0, 0, tiled=True)  38.5 us
    pallas_call x1, Pallas kernels, shards(): call(ffn_kernel, (steps // 2,), [tok_spec(2 * PER), tok_spec(2 * PER), mo...  25.6 us
    all_to_all x1, blocking collectives, swap(): return lax.all_to_all(array, axes, 0, 0, tiled=True)  22.5 us
    ppermute x11, starting transfers between devices, flip(): return lax.ppermute(array, 'core', [(0, 1), (1, 0)])  21.5 us
    ppermute x15, starting transfers between devices, shift(): return lax.ppermute(array, axis, [(i, (i + step) % 4) for i in range(4)])  15 us
    ppermute x2, starting transfers between devices, to_plane(): return lax.ppermute(array, ALL, pairs)  13.6 us
    ppermute x15, waiting for transfers between devices, shift(): return lax.ppermute(array, axis, [(i, (i + step) % 4) for i in range(4)])  11.4 us
    ppermute x2, waiting for transfers between devices, flip_x(): return lax.ppermute(array, 'x', [(i, i ^ 1) for i in range(4)])  9.52 us
  transfers between devices with their start and end apart: 36, of which 13 were waited for; matrix products, arithmetic and copies ran while one was open for 0% of the time, Pallas kernels for 21%

profile of v2, /device:TPU:1, one launch (start us, length us, event | category | flops | bytes accessed | tf_op | source)
XLA Modules:
  0.0 255.6 jit_solution(11180393822173295661)
XLA Ops:
  0.6 6.0 %collective-permute-start = (bf16[64,1024]{1,0:T(8,128)(2,1)}, bf16[64,1024]{1,0:T(8,128)(2,1)S(1)}, u32[]{:S(2)}, u32[]{:S(2)}) collective-permute-start(bf16[64,1024]{1,0:T(8,128)(2,1)} %bitcast.17), channel_id=1, source_target_pairs={{0,0},{1,64},{2,8},{3,72},{4,16},{5,80},{6,24},{7,88},{8,2},{9,66}... | collective-permute-start | bytes 393224 | tf_op jit(solution)/shard_map/logits/ppermute | solution.py:501
  6.7 5.2 %values.1 = bf16[16,64,512]{2,1,0:T(8,128)(2,1)} custom-call(s32[128]{0:T(128)} %lens_ref.9, bf16[16,64,512]{2,1,0:T(8,128)(2,1)} %tok_ref.7, bf16[512]{0:T(512)(128)(2,1)} %gain_ref.9, bf16[512,512]{1,0:T(8,128)(2,1)} %vw_ref.5), custom_call_target="tpu_custom_call" | custom-call | flops 1000000 | bytes 100000 | tf_op jit(solution)/shard_map/values/pallas_call | solution.py:573
  12.2 3.5 %collective-permute-done.1 = bf16[64,1024]{1,0:T(8,128)(2,1)S(1)} collective-permute-done((bf16[64,1024]{1,0:T(8,128)(2,1)S(1)}, bf16[64,1024]{1,0:T(8,128)(2,1)S(1)}, u32[]{:S(2)}, u32[]{:S(2)}) %collective-permute-start.1) | collective-permute-done | bytes 131104 | tf_op jit(solution)/shard_map/logits/ppermute | solution.py:494
  15.7 10.0 %all-to-all-start = ((bf16[16,64,512]{2,1,0:T(8,128)(2,1)}), bf16[16,64,512]{2,1,0:T(8,128)(2,1)}, u32[]{:S(2)}, u32[]{:S(2)}) async-start(bf16[16,64,512]{2,1,0:T(8,128)(2,1)} %values.1), calls=%async_computation | async-start | bytes 2097152 | tf_op jit(solution)/shard_map/logits/all_to_all | solution.py:509
  25.7 1.4 collective-permute-start.4
  27.1 1.8 collective-permute-start.3
  28.9 2.3 collective-permute-start.5
  31.2 6.1 %collective-permute-start.8 = (bf16[128,1024]{1,0:T(8,128)(2,1)S(1)}, bf16[128,1024]{1,0:T(8,128)(2,1)S(1)}, u32[]{:S(2)}, u32[]{:S(2)}) collective-permute-start(bf16[128,1024]{1,0:T(8,128)(2,1)S(1)} %collective-permute-done.4.refs_3_), channel_id=1, source_target_pairs={{0,1},{1,0},{2,3},{3,2},{4,5},{5,4},{6,7},{7,6},{8,9},{9,8},{10,11... | collective-permute-start | bytes 786440 | tf_op jit(solution)/shard_map/logits/ppermute | solution.py:490
  37.3 2.9 %collective-permute-start.7 = (bf16[128,1024]{1,0:T(8,128)(2,1)S(1)}, bf16[128,1024]{1,0:T(8,128)(2,1)S(1)}, u32[]{:S(2)}, u32[]{:S(2)}) collective-permute-start(bf16[128,1024]{1,0:T(8,128)(2,1)S(1)} %collective-permute-done.3.refs_2_), channel_id=1, source_target_pairs={{0,1},{1,0},{2,3},{3,2},{4,5},{5,4},{6,7},{7,6},{8,9},{9,8},{10,11... | collective-permute-start | bytes 786440 | tf_op jit(solution)/shard_map/logits/ppermute | solution.py:490
  40.2 1.3 collective-permute-done.2.refs_1_
  41.5 1.4 collective-permute-start.6
  43.0 0.7 copy-done.8
  43.7 0.7 copy-done.10
  44.5 7.2 %mix.1 = (bf16[1024,1024]{1,0:T(8,128)(2,1)}, f32[1024,512]{1,0:T(8,128)}, bf16[1024,512]{1,0:T(8,128)(2,1)}) custom-call(s32[128]{0:T(128)} %lens_ref.9, bf16[128,1024]{1,0:T(8,128)(2,1)} %copy-done.4, bf16[128,1024]{1,0:T(8,128)(2,1)} %copy-done.7, bf16[128,1024]{1,0:T(8,128)(2,1)} %copy-done.6, bf16[128,1024]{1,0:T(8,128)(2,1)} %copy-done.5, ...), custom_call_target="tpu_custom_call" | custom-call | flops 1000000 | bytes 100000 | tf_op jit(solution)/shard_map/mix/pallas_call | solution.py:595
  51.7 22.5 %all_to_all.35.mix_ref = bf16[16,64,512]{2,1,0:T(8,128)(2,1)} all-to-all(bf16[16,64,512]{2,1,0:T(8,128)(2,1)} %bitcast.9), channel_id=1, replica_groups=mesh['x'=4,'y'=4,'z'=4,'core'=2] {'x','y'}, dimensions={0} | all-to-all | bytes 2097152 | tf_op jit(solution)/shard_map/mix/all_to_all | solution.py:509
  74.2 25.6 %ffn.1 = (bf16[16,64,512]{2,1,0:T(8,128)(2,1)}, f32[1024,512]{1,0:T(8,128)}, bf16[16,64,512]{2,1,0:T(8,128)(2,1)}, bf16[4,1152,256]{2,1,0:T(8,128)(2,1)}, bf16[4,1152,256]{2,1,0:T(8,128)(2,1)}) custom-call(s32[128]{0:T(128)} %lens_ref.9, bf16[16,64,512]{2,1,0:T(8,128)(2,1)} %tok_ref.7, bf16[16,64,512]{2,1,0:T(8,128)(2,1)} %cot_ref.1, ...), custom_call_target="tpu_custom_call" | custom-call | flops 1000000 | bytes 100000 | tf_op jit(solution)/shard_map/ffn/pallas_call | solution.py:621
  99.8 2.3 collective-permute-start.9
  102.1 4.3 %all-to-all-start.2 = ((bf16[16,64,512]{2,1,0:T(8,128)(2,1)}), bf16[16,64,512]{2,1,0:T(8,128)(2,1)}, u32[]{:S(2)}, u32[]{:S(2)}) async-start(bf16[16,64,512]{2,1,0:T(8,128)(2,1)} %get-tuple-element.73), calls=%async_computation.2 | async-start | bytes 2097152 | tf_op jit(solution)/shard_map/ffn/all_to_all | solution.py:509
  106.6 5.0 %ffn_sum.3 = (bf16[1152,256]{1,0:T(8,128)(2,1)}, bf16[1152,256]{1,0:T(8,128)(2,1)}, bf16[1152,256]{1,0:T(8,128)(2,1)}, bf16[1152,256]{1,0:T(8,128)(2,1)}) custom-call(bf16[4,1152,256]{2,1,0:T(8,128)(2,1)} %get-tuple-element.74.own_ref, bf16[4,1152,256]{2,1,0:T(8,128)(2,1)} %collective-permute-done.9.got_ref), custom_call_target="tpu_custom_call" | custom-call | flops 1000000 | bytes 100000 | tf_op jit(solution)/shard_map/ffn_sum/pallas_call | solution.py:665
  112.0 1.6 collective-permute-start.12
  113.6 1.6 collective-permute-start.13
  115.2 9.1 %all-to-all-done.2 = bf16[16,64,512]{2,1,0:T(8,128)(2,1)} async-done(((bf16[16,64,512]{2,1,0:T(8,128)(2,1)}), bf16[16,64,512]{2,1,0:T(8,128)(2,1)}, u32[]{:S(2)}, u32[]{:S(2)}) %all-to-all-start.2) | async-done | bytes 1048608 | tf_op jit(solution)/shard_map/ffn/all_to_all | solution.py:509
  124.3 6.4 %unmix.1 = (bf16[1024,512]{1,0:T(8,128)(2,1)}, bf16[1024,512]{1,0:T(8,128)(2,1)}, bf16[1024,512]{1,0:T(8,128)(2,1)}) custom-call(bf16[1024,1024]{1,0:T(8,128)(2,1)} %get-tuple-element.72.exp_ref, bf16[1024,512]{1,0:T(8,128)(2,1)} %bitcast.3.gm_ref, f32[1024,512]{1,0:T(8,128)} %get-tuple-element.78.inv_ref, bf16[1024,512]{1,0:T(8,128)(2,1)} %get-tuple-element.70.mixed_ref), custom_call_target="tpu_custom_call" | custom-call | flops 1000000 | bytes 100000 | tf_op jit(solution)/shard_map/unmix/pallas_call | solution.py:681
  130.7 4.6 %all-to-all-start.3 = ((bf16[16,64,512]{2,1,0:T(8,128)(2,1)}), bf16[16,64,512]{2,1,0:T(8,128)(2,1)}, u32[]{:S(2)}, u32[]{:S(2)}) async-start(bf16[16,64,512]{2,1,0:T(8,128)(2,1)} %bitcast.15), calls=%async_computation.3 | async-start | bytes 2097152 | tf_op jit(solution)/shard_map/unmix/all_to_all | solution.py:509
  135.3 7.1 %scores.1 = (bf16[4,2,64,1024]{3,2,1,0:T(8,128)(2,1)}, bf16[4,2,64,1024]{3,2,1,0:T(8,128)(2,1)}) custom-call(s32[128]{0:T(128)} %lens_ref.9, bf16[1024,512]{1,0:T(8,128)(2,1)} %get-tuple-element.80.g_ref, bf16[1024,512]{1,0:T(8,128)(2,1)} %get-tuple-element.81.r_ref, bf16[1024,512]{1,0:T(8,128)(2,1)} %bitcast.1.refs_8_.val_ref), custom_call_target="tpu_custom_call" | custom-call | flops 1000000 | bytes 100000 | tf_op jit(solution)/shard_map/scores/pallas_call | solution.py:695
  142.4 1.1 collective-permute-start.10
  143.5 0.8 copy-done.18
  144.3 3.7 %ffn_sum.4 = bf16[1152,256]{1,0:T(8,128)(2,1)} custom-call(bf16[1152,256]{1,0:T(8,128)(2,1)} %get-tuple-element.88.refs_0_, bf16[1152,256]{1,0:T(8,128)(2,1)} %copy-done.18, bf16[1152,256]{1,0:T(8,128)(2,1)} %collective-permute-done.12.refs_2_, bf16[1152,256]{1,0:T(8,128)(2,1)} %collective-permute-done.13.refs_3_), custom_call_target="tpu_custom_call" | custom-call | flops 9999999827968 | bytes 1000000 | tf_op jit(solution)/shard_map/ffn_sum/pallas_call | solution.py:711
  148.0 3.6 %score_sum.4 = (bf16[2,64,1024]{2,1,0:T(8,128)(2,1)}, bf16[2,64,1024]{2,1,0:T(8,128)(2,1)}, bf16[2,64,1024]{2,1,0:T(8,128)(2,1)}, bf16[2,64,1024]{2,1,0:T(8,128)(2,1)}) custom-call(bf16[4,2,64,1024]{3,2,1,0:T(8,128)(2,1)} %get-tuple-element.92.own_ref, bf16[4,2,64,1024]{3,2,1,0:T(8,128)(2,1)} %collective-permute-done.10.got_ref), custom_call_target="tpu_custom_call" | custom-call | flops 1000000 | bytes 100000 | tf_op jit(solution)/shard_map/score_sum/pallas_call | solution.py:665
  152.0 1.6 collective-permute-start.15
  153.5 1.6 collective-permute-start.16
  155.1 6.1 %value_grad.1 = (bf16[1024,512]{1,0:T(8,128)(2,1)}, bf16[16,136,256]{2,1,0:T(8,128)(2,1)}) custom-call(s32[128]{0:T(128)} %lens_ref.9, bf16[16,64,512]{2,1,0:T(8,128)(2,1)} %tok_ref.7, bf16[16,64,512]{2,1,0:T(8,128)(2,1)} %all-to-all-done.3.vg_ref, bf16[512]{0:T(512)(128)(2,1)} %gain_ref.9, bf16[16,72,256]{2,1,0:T(8,128)(2,1)} %bitcast.16), custom_call_target="tpu_custom_call" | custom-call | flops 1000000 | bytes 100000 | tf_op jit(solution)/shard_map/value_grad/pallas_call | solution.py:733
  161.3 6.9 %all-to-all-start.4 = ((bf16[16,136,256]{2,1,0:T(8,128)(2,1)}), bf16[16,136,256]{2,1,0:T(8,128)(2,1)}, u32[]{:S(2)}, u32[]{:S(2)}) async-start(bf16[16,136,256]{2,1,0:T(8,128)(2,1)} %get-tuple-element.101), calls=%async_computation.4 | async-start | bytes 2228224 | tf_op jit(solution)/shard_map/value_grad/all_to_all | solution.py:509
  168.9 0.7 copy-done.21
  169.6 2.0 score_sum.5
  171.7 1.3 collective-permute-start.17
  173.0 5.2 %input_grad.1 = f32[16,64,512]{2,1,0:T(8,128)} custom-call(bf16[16,64,512]{2,1,0:T(8,128)(2,1)} %tok_ref.7, bf16[1024,512]{1,0:T(8,128)(2,1)} %get-tuple-element.96.vgrad_ref, f32[1024,512]{1,0:T(8,128)} %get-tuple-element.107.gr_ref, bf16[512]{0:T(512)(128)(2,1)} %gain_ref.9, bf16[512,512]{1,0:T(8,128)(2,1)} %vw_ref.5), custom_call_target="tpu_custom_call" | custom-call | flops 1000000 | bytes 100000 | tf_op jit(solution)/shard_map/input_grad/pallas_call | solution.py:760
  178.2 6.0 %collective-permute-done.17.refs_1_ = bf16[64,1024]{1,0:T(8,128)(2,1)S(1)} collective-permute-done((bf16[64,1024]{1,0:T(8,128)(2,1)}, bf16[64,1024]{1,0:T(8,128)(2,1)S(1)}, u32[]{:S(2)}, u32[]{:S(2)}) %collective-permute-start.17) | collective-permute-done | bytes 131104 | tf_op jit(solution)/shard_map/score_sum/ppermute | solution.py:494
  184.8 1.7 score_sum.6
  186.5 2.2 joint_sum.1
  188.7 6.2 %all-to-all-start.5 = ((bf16[16,72,256]{2,1,0:T(8,128)(2,1)}), bf16[16,72,256]{2,1,0:T(8,128)(2,1)S(1)}, u32[]{:S(2)}, u32[]{:S(2)}) async-start(bf16[16,72,256]{2,1,0:T(8,128)(2,1)} %get-tuple-element.113), calls=%async_computation.5 | async-start | bytes 1179648 | tf_op jit(solution)/shard_map/ffn_sum/all_to_all | solution.py:509
  194.9 2.3 collective-permute-start.18
  197.1 1.1 collective-permute-done.18.refs_1_
  198.8 1.4 value_sum.3.refs_0_
  200.3 1.6 collective-permute-start.20
  201.9 0.7 collective-permute-start.19
  202.6 0.9 collective-permute-done.21.refs_3_
  203.5 1.6 collective-permute-done.20.refs_2_
  205.1 1.4 collective-permute-done.19.refs_1_
  207.1 1.7 value_sum.4
  208.8 1.1 collective-permute-start.25
  210.0 1.2 collective-permute-start.24
  211.2 6.6 %all-to-all-start.6 = ((bf16[16,64,256]{2,1,0:T(8,128)(2,1)}), bf16[16,64,256]{2,1,0:T(8,128)(2,1)}, u32[]{:S(2)}, u32[]{:S(2)}) async-start(bf16[16,64,256]{2,1,0:T(8,128)(2,1)} %value_sum.4), calls=%async_computation.6 | async-start | bytes 1048576 | tf_op jit(solution)/shard_map/value_sum/all_to_all | solution.py:509
  217.8 7.5 %collective-permute-start.22 = (bf16[64,1024]{1,0:T(8,128)(2,1)S(1)}, bf16[64,1024]{1,0:T(8,128)(2,1)S(1)}, u32[]{:S(2)}, u32[]{:S(2)}) collective-permute-start(bf16[64,1024]{1,0:T(8,128)(2,1)S(1)} %copy-done.11), channel_id=1, source_target_pairs={{0,0},{64,1},{8,2},{72,3},{16,4},{80,5},{24,6},{88,7},{2,8},{66,9}... | collective-permute-start | bytes 393224 | tf_op jit(solution)/shard_map/score_sum/ppermute | solution.py:501
  225.3 4.1 %collective-permute-done.22.part_ref = bf16[64,1024]{1,0:T(8,128)(2,1)S(1)} collective-permute-done((bf16[64,1024]{1,0:T(8,128)(2,1)S(1)}, bf16[64,1024]{1,0:T(8,128)(2,1)S(1)}, u32[]{:S(2)}, u32[]{:S(2)}) %collective-permute-start.22) | collective-permute-done | bytes 131104 | tf_op jit(solution)/shard_map/score_sum/ppermute | solution.py:501
  230.1 1.8 score_sum.7
  231.9 2.3 value_sum.5
  234.2 6.1 %collective-permute-done.23.refs_1_ = bf16[1152,256]{1,0:T(8,128)(2,1)} collective-permute-done((bf16[1152,256]{1,0:T(8,128)(2,1)S(1)}, bf16[1152,256]{1,0:T(8,128)(2,1)}, u32[]{:S(2)}, u32[]{:S(2)}) %collective-permute-start.23) | collective-permute-done | bytes 589856 | tf_op jit(solution)/shard_map/ffn_sum/ppermute | solution.py:486
  240.4 2.6 %collective-permute-start.26 = (bf16[1152,256]{1,0:T(8,128)(2,1)S(1)}, bf16[1152,256]{1,0:T(8,128)(2,1)S(1)}, u32[]{:S(2)}, u32[]{:S(2)}) collective-permute-start(bf16[1152,256]{1,0:T(8,128)(2,1)S(1)} %bitcast.13), channel_id=1, source_target_pairs={{0,1},{1,0},{2,3},{3,2},{4,5},{5,4},{6,7},{7,6},{8,9},{9,8},{10,11... | collective-permute-start | bytes 1769480 | tf_op jit(solution)/shard_map/ffn_sum/ppermute | solution.py:490
  243.5 1.9 collective-permute-done.26.refs_4_
  245.4 0.8 copy-done.1
  246.3 0.8 copy-done.2
  247.4 0.8 copy-done.3
  248.2 7.2 %ffn_sum.5 = (f32[2048,512]{1,0:T(8,128)}, f32[512,2048]{1,0:T(8,128)}, f32[512,512]{1,0:T(8,128)}, f32[1,512]{1,0:T(1,128)}) custom-call(bf16[1152,256]{1,0:T(8,128)(2,1)} %bitcast.14, bf16[1152,256]{1,0:T(8,128)(2,1)} %collective-permute-done.23.refs_1_, bf16[1152,256]{1,0:T(8,128)(2,1)} %collective-permute-done.24.refs_2_, ...), custom_call_target="tpu_custom_call" | custom-call | flops 1000000 | bytes 100000 | tf_op jit(solution)/shard_map/ffn_sum/pallas_call | solution.py:853
  (73 shorter events, 5.6 us)
Async XLA Ops:
  0.6 11.2 %collective-permute-start = (bf16[64,1024]{1,0:T(8,128)(2,1)}, bf16[64,1024]{1,0:T(8,128)(2,1)S(1)}, u32[]{:S(2)}, u32[]{:S(2)}) collective-permute-start(bf16[64,1024]{1,0:T(8,128)(2,1)} %bitcast.17), channel_id=1, source_target_pairs={{0,0},{1,64},{2,8},{3,72},{4,16},{5,80},{6,24},{7,88},{8,2},{9,66}... | collective-permute-start | bytes 393224 | tf_op jit(solution)/shard_map/logits/ppermute | solution.py:501
  11.9 3.8 %collective-permute-start.1 = (bf16[64,1024]{1,0:T(8,128)(2,1)S(1)}, bf16[64,1024]{1,0:T(8,128)(2,1)S(1)}, u32[]{:S(2)}, u32[]{:S(2)}) collective-permute-start(bf16[64,1024]{1,0:T(8,128)(2,1)S(1)} %collective-permute-done), channel_id=1, source_target_pairs={{0,32},{32,0},{64,96},{96,64},{1,33},{33,1},{65,97},{97,65},{2,34}... | collective-permute-start | bytes 393224 | tf_op jit(solution)/shard_map/logits/ppermute | solution.py:494
  15.7 28.8 %all-to-all-start = ((bf16[16,64,512]{2,1,0:T(8,128)(2,1)}), bf16[16,64,512]{2,1,0:T(8,128)(2,1)}, u32[]{:S(2)}, u32[]{:S(2)}) async-start(bf16[16,64,512]{2,1,0:T(8,128)(2,1)} %values.1), calls=%async_computation | async-start | bytes 2097152 | tf_op jit(solution)/shard_map/logits/all_to_all | solution.py:509
  25.7 18.7 %copy-start.4 = (bf16[128,1024]{1,0:T(8,128)(2,1)}, bf16[128,1024]{1,0:T(8,128)(2,1)S(1)}, u32[]{:S(2)}) copy-start(bf16[128,1024]{1,0:T(8,128)(2,1)S(1)} %constant_dynamic-update-slice_fusion.refs_0_) | copy-start | bytes 786436
  25.7 5.5 %collective-permute-start.4 = (bf16[128,1024]{1,0:T(8,128)(2,1)S(1)}, bf16[128,1024]{1,0:T(8,128)(2,1)S(1)}, u32[]{:S(2)}, u32[]{:S(2)}) collective-permute-start(bf16[128,1024]{1,0:T(8,128)(2,1)S(1)} %constant_dynamic-update-slice_fusion.refs_0_), channel_id=1, source_target_pairs={{0,6},{2,0},{4,2},{6,4},{1,7},{3,1},{5,3},{7,5},{8,14},{10,8},{12,... | collective-permute-start | bytes 786440 | tf_op jit(solution)/shard_map/logits/ppermute | solution.py:486
  27.1 10.2 %collective-permute-start.3 = (bf16[128,1024]{1,0:T(8,128)(2,1)S(1)}, bf16[128,1024]{1,0:T(8,128)(2,1)S(1)}, u32[]{:S(2)}, u32[]{:S(2)}) collective-permute-start(bf16[128,1024]{1,0:T(8,128)(2,1)S(1)} %constant_dynamic-update-slice_fusion.refs_0_), channel_id=1, source_target_pairs={{0,4},{2,6},{4,0},{6,2},{1,5},{3,7},{5,1},{7,3},{8,12},{10,14},{12... | collective-permute-start | bytes 786440 | tf_op jit(solution)/shard_map/logits/ppermute | solution.py:486
  28.9 12.6 %collective-permute-start.2 = (bf16[128,1024]{1,0:T(8,128)(2,1)S(1)}, bf16[128,1024]{1,0:T(8,128)(2,1)S(1)}, u32[]{:S(2)}, u32[]{:S(2)}) collective-permute-start(bf16[128,1024]{1,0:T(8,128)(2,1)S(1)} %constant_dynamic-update-slice_fusion.refs_0_), channel_id=1, source_target_pairs={{0,2},{2,4},{4,6},{6,0},{1,3},{3,5},{5,7},{7,1},{8,10},{10,12},{12... | collective-permute-start | bytes 786440 | tf_op jit(solution)/shard_map/logits/ppermute | solution.py:486
  28.9 14.0 %collective-permute-start.5 = (bf16[128,1024]{1,0:T(8,128)(2,1)S(1)}, bf16[128,1024]{1,0:T(8,128)(2,1)S(1)}, u32[]{:S(2)}, u32[]{:S(2)}) collective-permute-start(bf16[128,1024]{1,0:T(8,128)(2,1)S(1)} %constant_dynamic-update-slice_fusion.refs_0_), channel_id=1, source_target_pairs={{0,1},{1,0},{2,3},{3,2},{4,5},{5,4},{6,7},{7,6},{8,9},{9,8},{10,11... | collective-permute-start | bytes 786440 | tf_op jit(solution)/shard_map/logits/ppermute | solution.py:490
  31.2 13.3 %copy-start.5 = (bf16[128,1024]{1,0:T(8,128)(2,1)}, bf16[128,1024]{1,0:T(8,128)(2,1)S(1)}, u32[]{:S(2)}) copy-start(bf16[128,1024]{1,0:T(8,128)(2,1)S(1)} %collective-permute-done.4.refs_3_) | copy-start | bytes 786436
  31.2 11.7 %collective-permute-start.8 = (bf16[128,1024]{1,0:T(8,128)(2,1)S(1)}, bf16[128,1024]{1,0:T(8,128)(2,1)S(1)}, u32[]{:S(2)}, u32[]{:S(2)}) collective-permute-start(bf16[128,1024]{1,0:T(8,128)(2,1)S(1)} %collective-permute-done.4.refs_3_), channel_id=1, source_target_pairs={{0,1},{1,0},{2,3},{3,2},{4,5},{5,4},{6,7},{7,6},{8,9},{9,8},{10,11... | collective-permute-start | bytes 786440 | tf_op jit(solution)/shard_map/logits/ppermute | solution.py:490
  37.3 7.1 %copy-start.6 = (bf16[128,1024]{1,0:T(8,128)(2,1)}, bf16[128,1024]{1,0:T(8,128)(2,1)S(1)}, u32[]{:S(2)}) copy-start(bf16[128,1024]{1,0:T(8,128)(2,1)S(1)} %collective-permute-done.3.refs_2_) | copy-start | bytes 786436
  37.3 5.6 %collective-permute-start.7 = (bf16[128,1024]{1,0:T(8,128)(2,1)S(1)}, bf16[128,1024]{1,0:T(8,128)(2,1)S(1)}, u32[]{:S(2)}, u32[]{:S(2)}) collective-permute-start(bf16[128,1024]{1,0:T(8,128)(2,1)S(1)} %collective-permute-done.3.refs_2_), channel_id=1, source_target_pairs={{0,1},{1,0},{2,3},{3,2},{4,5},{5,4},{6,7},{7,6},{8,9},{9,8},{10,11... | collective-permute-start | bytes 786440 | tf_op jit(solution)/shard_map/logits/ppermute | solution.py:490
  41.5 1.4 copy-start.7
  41.5 2.9 %collective-permute-start.6 = (bf16[128,1024]{1,0:T(8,128)(2,1)S(1)}, bf16[128,1024]{1,0:T(8,128)(2,1)}, u32[]{:S(2)}, u32[]{:S(2)}) collective-permute-start(bf16[128,1024]{1,0:T(8,128)(2,1)S(1)} %collective-permute-done.2.refs_1_), channel_id=1, source_target_pairs={{0,1},{1,0},{2,3},{3,2},{4,5},{5,4},{6,7},{7,6},{8,9},{9,8},{10,11... | collective-permute-start | bytes 786440 | tf_op jit(solution)/shard_map/logits/ppermute | solution.py:490
  42.9 0.7 copy-start.8
  42.9 0.8 copy-start.9
  43.7 0.7 copy-start.10
  99.8 6.8 %collective-permute-start.9 = (bf16[4,1152,256]{2,1,0:T(8,128)(2,1)}, bf16[4,1152,256]{2,1,0:T(8,128)(2,1)}, u32[]{:S(2)}, u32[]{:S(2)}) collective-permute-start(bf16[4,1152,256]{2,1,0:T(8,128)(2,1)} %get-tuple-element.75), channel_id=1, source_target_pairs={{0,1},{1,0},{2,3},{3,2},{4,5},{5,4},{6,7},{7,6},{8,9},{9,8},{10,11... | collective-permute-start | bytes 7077896 | tf_op jit(solution)/shard_map/ffn_sum/ppermute | solution.py:490
  102.1 22.2 %all-to-all-start.2 = ((bf16[16,64,512]{2,1,0:T(8,128)(2,1)}), bf16[16,64,512]{2,1,0:T(8,128)(2,1)}, u32[]{:S(2)}, u32[]{:S(2)}) async-start(bf16[16,64,512]{2,1,0:T(8,128)(2,1)} %get-tuple-element.73), calls=%async_computation.2 | async-start | bytes 2097152 | tf_op jit(solution)/shard_map/ffn/all_to_all | solution.py:509
  111.7 31.8 %collective-permute-start.11 = (bf16[1152,256]{1,0:T(8,128)(2,1)}, bf16[1152,256]{1,0:T(8,128)(2,1)S(1)}, u32[]{:S(2)}, u32[]{:S(2)}) collective-permute-start(bf16[1152,256]{1,0:T(8,128)(2,1)} %get-tuple-element.85), channel_id=1, source_target_pairs={{0,2},{2,4},{4,6},{6,0},{1,3},{3,5},{5,7},{7,1},{8,10},{10,12},{12... | collective-permute-start | bytes 1769480 | tf_op jit(solution)/shard_map/ffn_sum/ppermute | solution.py:486
  112.0 31.5 %collective-permute-start.12 = (bf16[1152,256]{1,0:T(8,128)(2,1)}, bf16[1152,256]{1,0:T(8,128)(2,1)}, u32[]{:S(2)}, u32[]{:S(2)}) collective-permute-start(bf16[1152,256]{1,0:T(8,128)(2,1)} %get-tuple-element.86), channel_id=1, source_target_pairs={{0,4},{2,6},{4,0},{6,2},{1,5},{3,7},{5,1},{7,3},{8,12},{10,14},{12... | collective-permute-start | bytes 1769480 | tf_op jit(solution)/shard_map/ffn_sum/ppermute | solution.py:486
  113.6 29.9 %collective-permute-start.13 = (bf16[1152,256]{1,0:T(8,128)(2,1)}, bf16[1152,256]{1,0:T(8,128)(2,1)}, u32[]{:S(2)}, u32[]{:S(2)}) collective-permute-start(bf16[1152,256]{1,0:T(8,128)(2,1)} %get-tuple-element.87), channel_id=1, source_target_pairs={{0,6},{2,0},{4,2},{6,4},{1,7},{3,1},{5,3},{7,5},{8,14},{10,8},{12,... | collective-permute-start | bytes 1769480 | tf_op jit(solution)/shard_map/ffn_sum/ppermute | solution.py:486
  130.7 24.4 %all-to-all-start.3 = ((bf16[16,64,512]{2,1,0:T(8,128)(2,1)}), bf16[16,64,512]{2,1,0:T(8,128)(2,1)}, u32[]{:S(2)}, u32[]{:S(2)}) async-start(bf16[16,64,512]{2,1,0:T(8,128)(2,1)} %bitcast.15), calls=%async_computation.3 | async-start | bytes 2097152 | tf_op jit(solution)/shard_map/unmix/all_to_all | solution.py:509
  142.4 5.6 %collective-permute-start.10 = (bf16[4,2,64,1024]{3,2,1,0:T(8,128)(2,1)}, bf16[4,2,64,1024]{3,2,1,0:T(8,128)(2,1)}, u32[]{:S(2)}, u32[]{:S(2)}) collective-permute-start(bf16[4,2,64,1024]{3,2,1,0:T(8,128)(2,1)} %get-tuple-element.84), channel_id=1, source_target_pairs={{0,1},{1,0},{2,3},{3,2},{4,5},{5,4},{6,7},{7,6},{8,9},{9,8},{10,11... | collective-permute-start | bytes 3145736 | tf_op jit(solution)/shard_map/scores/ppermute | solution.py:490
  143.5 0.8 copy-start.18
  151.6 16.5 %collective-permute-start.14 = (bf16[2,64,1024]{2,1,0:T(8,128)(2,1)}, bf16[2,64,1024]{2,1,0:T(8,128)(2,1)S(1)}, u32[]{:S(2)}, u32[]{:S(2)}) collective-permute-start(bf16[2,64,1024]{2,1,0:T(8,128)(2,1)} %get-tuple-element.98), channel_id=1, source_target_pairs={{0,2},{2,4},{4,6},{6,0},{1,3},{3,5},{5,7},{7,1},{8,10},{10,12},{12... | collective-permute-start | bytes 786440 | tf_op jit(solution)/shard_map/score_sum/ppermute | solution.py:486
  152.0 16.2 %collective-permute-start.15 = (bf16[2,64,1024]{2,1,0:T(8,128)(2,1)}, bf16[2,64,1024]{2,1,0:T(8,128)(2,1)S(1)}, u32[]{:S(2)}, u32[]{:S(2)}) collective-permute-start(bf16[2,64,1024]{2,1,0:T(8,128)(2,1)} %get-tuple-element.99), channel_id=1, source_target_pairs={{0,4},{2,6},{4,0},{6,2},{1,5},{3,7},{5,1},{7,3},{8,12},{10,14},{12... | collective-permute-start | bytes 786440 | tf_op jit(solution)/shard_map/score_sum/ppermute | solution.py:486
  153.5 14.6 %collective-permute-start.16 = (bf16[2,64,1024]{2,1,0:T(8,128)(2,1)}, bf16[2,64,1024]{2,1,0:T(8,128)(2,1)S(1)}, u32[]{:S(2)}, u32[]{:S(2)}) collective-permute-start(bf16[2,64,1024]{2,1,0:T(8,128)(2,1)} %get-tuple-element.100), channel_id=1, source_target_pairs={{0,6},{2,0},{4,2},{6,4},{1,7},{3,1},{5,3},{7,5},{8,14},{10,8},{12,... | collective-permute-start | bytes 786440 | tf_op jit(solution)/shard_map/score_sum/ppermute | solution.py:486
  161.3 25.2 %all-to-all-start.4 = ((bf16[16,136,256]{2,1,0:T(8,128)(2,1)}), bf16[16,136,256]{2,1,0:T(8,128)(2,1)}, u32[]{:S(2)}, u32[]{:S(2)}) async-start(bf16[16,136,256]{2,1,0:T(8,128)(2,1)} %get-tuple-element.101), calls=%async_computation.4 | async-start | bytes 2228224 | tf_op jit(solution)/shard_map/value_grad/all_to_all | solution.py:509
  168.1 0.7 copy-start.19
  168.2 0.8 copy-start.20
  168.9 0.7 copy-start.21
  171.7 12.5 %collective-permute-start.17 = (bf16[64,1024]{1,0:T(8,128)(2,1)}, bf16[64,1024]{1,0:T(8,128)(2,1)S(1)}, u32[]{:S(2)}, u32[]{:S(2)}) collective-permute-start(bf16[64,1024]{1,0:T(8,128)(2,1)} %get-tuple-element.108), channel_id=1, source_target_pairs={{0,32},{32,0},{64,96},{96,64},{1,33},{33,1},{65,97},{97,65},{2,34}... | collective-permute-start | bytes 393224 | tf_op jit(solution)/shard_map/score_sum/ppermute | solution.py:494
  184.2 0.7 copy-start.12
  186.5 31.3 %copy-start.11 = (bf16[64,1024]{1,0:T(8,128)(2,1)S(1)}, bf16[64,1024]{1,0:T(8,128)(2,1)}, u32[]{:S(2)}) copy-start(bf16[64,1024]{1,0:T(8,128)(2,1)} %score_sum.6) | copy-start | bytes 393220
  188.7 20.1 %all-to-all-start.5 = ((bf16[16,72,256]{2,1,0:T(8,128)(2,1)}), bf16[16,72,256]{2,1,0:T(8,128)(2,1)S(1)}, u32[]{:S(2)}, u32[]{:S(2)}) async-start(bf16[16,72,256]{2,1,0:T(8,128)(2,1)} %get-tuple-element.113), calls=%async_computation.5 | async-start | bytes 1179648 | tf_op jit(solution)/shard_map/ffn_sum/all_to_all | solution.py:509
  194.9 3.3 %collective-permute-start.18 = (bf16[64,256]{1,0:T(8,128)(2,1)}, bf16[64,256]{1,0:T(8,128)(2,1)S(1)}, u32[]{:S(2)}, u32[]{:S(2)}) collective-permute-start(bf16[64,256]{1,0:T(8,128)(2,1)} %get-tuple-element.112.refs_0_), channel_id=1, source_target_pairs={{0,1},{1,0},{2,3},{3,2},{4,5},{5,4},{6,7},{7,6},{8,9},{9,8},{10,11... | collective-permute-start | bytes 98312 | tf_op jit(solution)/shard_map/value_sum/ppermute | solution.py:490
  198.2 0.6 copy-start.17
  200.2 3.3 %collective-permute-start.21 = (bf16[64,256]{1,0:T(8,128)(2,1)}, bf16[64,256]{1,0:T(8,128)(2,1)S(1)}, u32[]{:S(2)}, u32[]{:S(2)}) collective-permute-start(bf16[64,256]{1,0:T(8,128)(2,1)} %value_sum.3.refs_0_), channel_id=1, source_target_pairs={{0,6},{2,0},{4,2},{6,4},{1,7},{3,1},{5,3},{7,5},{8,14},{10,8},{12,... | collective-permute-start | bytes 98312 | tf_op jit(solution)/shard_map/value_sum/ppermute | solution.py:486
  200.3 4.8 %collective-permute-start.20 = (bf16[64,256]{1,0:T(8,128)(2,1)}, bf16[64,256]{1,0:T(8,128)(2,1)S(1)}, u32[]{:S(2)}, u32[]{:S(2)}) collective-permute-start(bf16[64,256]{1,0:T(8,128)(2,1)} %value_sum.3.refs_0_), channel_id=1, source_target_pairs={{0,4},{2,6},{4,0},{6,2},{1,5},{3,7},{5,1},{7,3},{8,12},{10,14},{12... | collective-permute-start | bytes 98312 | tf_op jit(solution)/shard_map/value_sum/ppermute | solution.py:486
  201.9 4.6 %collective-permute-start.19 = (bf16[64,256]{1,0:T(8,128)(2,1)}, bf16[64,256]{1,0:T(8,128)(2,1)S(1)}, u32[]{:S(2)}, u32[]{:S(2)}) collective-permute-start(bf16[64,256]{1,0:T(8,128)(2,1)} %value_sum.3.refs_0_), channel_id=1, source_target_pairs={{0,2},{2,4},{4,6},{6,0},{1,3},{3,5},{5,7},{7,1},{8,10},{10,12},{12... | collective-permute-start | bytes 98312 | tf_op jit(solution)/shard_map/value_sum/ppermute | solution.py:486
  203.5 3.0 %copy-start.14 = (bf16[64,256]{1,0:T(8,128)(2,1)}, bf16[64,256]{1,0:T(8,128)(2,1)S(1)}, u32[]{:S(2)}) copy-start(bf16[64,256]{1,0:T(8,128)(2,1)S(1)} %collective-permute-done.21.refs_3_) | copy-start | bytes 98308
  205.1 1.4 copy-start.15
  206.5 0.6 copy-start.16
  208.8 39.4 %copy-start = (bf16[16,72,256]{2,1,0:T(8,128)(2,1)}, bf16[16,72,256]{2,1,0:T(8,128)(2,1)S(1)}, u32[]{:S(2)}) copy-start(bf16[16,72,256]{2,1,0:T(8,128)(2,1)S(1)} %all-to-all-done.5) | copy-start | bytes 1769476
  208.8 25.4 %collective-permute-start.25 = (bf16[1152,256]{1,0:T(8,128)(2,1)S(1)}, bf16[1152,256]{1,0:T(8,128)(2,1)}, u32[]{:S(2)}, u32[]{:S(2)}) collective-permute-start(bf16[1152,256]{1,0:T(8,128)(2,1)S(1)} %bitcast.10), channel_id=1, source_target_pairs={{0,6},{2,0},{4,2},{6,4},{1,7},{3,1},{5,3},{7,5},{8,14},{10,8},{12,... | collective-permute-start | bytes 1769480 | tf_op jit(solution)/shard_map/ffn_sum/ppermute | solution.py:486
  210.0 24.3 %collective-permute-start.24 = (bf16[1152,256]{1,0:T(8,128)(2,1)S(1)}, bf16[1152,256]{1,0:T(8,128)(2,1)}, u32[]{:S(2)}, u32[]{:S(2)}) collective-permute-start(bf16[1152,256]{1,0:T(8,128)(2,1)S(1)} %bitcast.11), channel_id=1, source_target_pairs={{0,4},{2,6},{4,0},{6,2},{1,5},{3,7},{5,1},{7,3},{8,12},{10,14},{12... | collective-permute-start | bytes 1769480 | tf_op jit(solution)/shard_map/ffn_sum/ppermute | solution.py:486
  211.2 29.2 %collective-permute-start.23 = (bf16[1152,256]{1,0:T(8,128)(2,1)S(1)}, bf16[1152,256]{1,0:T(8,128)(2,1)}, u32[]{:S(2)}, u32[]{:S(2)}) collective-permute-start(bf16[1152,256]{1,0:T(8,128)(2,1)S(1)} %bitcast.12), channel_id=1, source_target_pairs={{0,2},{2,4},{4,6},{6,0},{1,3},{3,5},{5,7},{7,1},{8,10},{10,12},{12... | collective-permute-start | bytes 1769480 | tf_op jit(solution)/shard_map/ffn_sum/ppermute | solution.py:486
  211.2 20.8 %all-to-all-start.6 = ((bf16[16,64,256]{2,1,0:T(8,128)(2,1)}), bf16[16,64,256]{2,1,0:T(8,128)(2,1)}, u32[]{:S(2)}, u32[]{:S(2)}) async-start(bf16[16,64,256]{2,1,0:T(8,128)(2,1)} %value_sum.4), calls=%async_computation.6 | async-start | bytes 1048576 | tf_op jit(solution)/shard_map/value_sum/all_to_all | solution.py:509
  217.8 11.7 %collective-permute-start.22 = (bf16[64,1024]{1,0:T(8,128)(2,1)S(1)}, bf16[64,1024]{1,0:T(8,128)(2,1)S(1)}, u32[]{:S(2)}, u32[]{:S(2)}) collective-permute-start(bf16[64,1024]{1,0:T(8,128)(2,1)S(1)} %copy-done.11), channel_id=1, source_target_pairs={{0,0},{64,1},{8,2},{72,3},{16,4},{80,5},{24,6},{88,7},{2,8},{66,9}... | collective-permute-start | bytes 393224 | tf_op jit(solution)/shard_map/score_sum/ppermute | solution.py:501
  229.4 0.7 copy-start.13
  240.4 5.1 %collective-permute-start.26 = (bf16[1152,256]{1,0:T(8,128)(2,1)S(1)}, bf16[1152,256]{1,0:T(8,128)(2,1)S(1)}, u32[]{:S(2)}, u32[]{:S(2)}) collective-permute-start(bf16[1152,256]{1,0:T(8,128)(2,1)S(1)} %bitcast.13), channel_id=1, source_target_pairs={{0,1},{1,0},{2,3},{3,2},{4,5},{5,4},{6,7},{7,6},{8,9},{9,8},{10,11... | collective-permute-start | bytes 1769480 | tf_op jit(solution)/shard_map/ffn_sum/ppermute | solution.py:490
  243.0 3.3 %collective-permute-start.27 = (bf16[1152,256]{1,0:T(8,128)(2,1)}, bf16[1152,256]{1,0:T(8,128)(2,1)S(1)}, u32[]{:S(2)}, u32[]{:S(2)}) collective-permute-start(bf16[1152,256]{1,0:T(8,128)(2,1)} %collective-permute-done.23.refs_1_), channel_id=1, source_target_pairs={{0,1},{1,0},{2,3},{3,2},{4,5},{5,4},{6,7},{7,6},{8,9},{9,8},{10,11... | collective-permute-start | bytes 1769480 | tf_op jit(solution)/shard_map/ffn_sum/ppermute | solution.py:490
  243.0 4.4 %collective-permute-start.28 = (bf16[1152,256]{1,0:T(8,128)(2,1)}, bf16[1152,256]{1,0:T(8,128)(2,1)S(1)}, u32[]{:S(2)}, u32[]{:S(2)}) collective-permute-start(bf16[1152,256]{1,0:T(8,128)(2,1)} %collective-permute-done.24.refs_2_), channel_id=1, source_target_pairs={{0,1},{1,0},{2,3},{3,2},{4,5},{5,4},{6,7},{7,6},{8,9},{9,8},{10,11... | collective-permute-start | bytes 1769480 | tf_op jit(solution)/shard_map/ffn_sum/ppermute | solution.py:490
  243.5 4.7 %collective-permute-start.29 = (bf16[1152,256]{1,0:T(8,128)(2,1)}, bf16[1152,256]{1,0:T(8,128)(2,1)}, u32[]{:S(2)}, u32[]{:S(2)}) collective-permute-start(bf16[1152,256]{1,0:T(8,128)(2,1)} %collective-permute-done.25.refs_3_), channel_id=1, source_target_pairs={{0,1},{1,0},{2,3},{3,2},{4,5},{5,4},{6,7},{7,6},{8,9},{9,8},{10,11... | collective-permute-start | bytes 1769480 | tf_op jit(solution)/shard_map/ffn_sum/ppermute | solution.py:490
  245.4 0.8 copy-start.1
  246.3 0.8 copy-start.2
  247.4 0.8 copy-start.3
